TPU v7x, 512 devices: a whole 4x8x8 slice. The times are simulated.
512 devices in a mesh: row: 4 (over z_lo), col: 8 (over x, core), dev: 16 (over z_hi, y).
Axes of the slice: x: 4, y: 8, z: 8 (z_hi: 2, z_lo: 4; z = z_hi * 4 + z_lo), core: 2. Of those that a mesh axis runs over, the one named last changes fastest.
Arguments:
- train_states: bfloat16 [512, 2, 262144], P(('row', 'col'), None, 'dev'), may hold values from -120 to 120, as said below
- test_states: bfloat16 [768, 2, 262144], P(('col', 'row'), None, 'dev'), may hold values from -120 to 120, as said below
Outputs:
- kernel: float32 [512, 768], P('row', 'col')
Inputs may be any that keep to these rules, and one draw needn't show every extreme that they name: `train_states`: unnormalized states. `test_states`: unnormalized states.
All inputs are finite; a program needn't handle non-finite values.
Results may differ from a plain program's by a relative error of at most 0.0003.
Values may be sent and summed in bfloat16 or wider, within the bound.
No kernel may reach another device: no remote copies, remote signals or barrier semaphores. Data moves between devices by JAX's collectives and lax.ppermute only.
A program may use at most 64 MiB of HBM per device.

v0:
```python
import jax
import jax.numpy as jnp
from jax import lax
from jax.sharding import PartitionSpec as P

AMPS = 262144


def pair_terms(left, right):
    product = jnp.einsum("bpl,cql->bpcq", left, right, preferred_element_type=jnp.float32)
    return product


def self_norms(states):
    return jnp.einsum("bpl,bpl->b", states, states, preferred_element_type=jnp.float32)


def per_device(train_states, test_states):
    test_panel = lax.all_gather(test_states, "row", axis=0, tiled=True)
    piece = lax.all_gather(train_states, "col", axis=0, tiled=True)
    intersection = pair_terms(piece, test_panel)
    norm_rows = self_norms(piece)
    intersection, train_norm = (intersection, norm_rows)
    test_norm = self_norms(test_panel)
    real_part = intersection[:, 0, :, 0] + intersection[:, 1, :, 1]
    imag_part = intersection[:, 0, :, 1] - intersection[:, 1, :, 0]
    real_part, imag_part, train_norm, test_norm = lax.psum(
        (real_part, imag_part, train_norm, test_norm), "dev"
    )
    return (
        float(AMPS)
        * (real_part * real_part + imag_part * imag_part)
        / (train_norm[:, None] * test_norm[None, :])
    )


def solution(mesh):
    placed = (P(("row", "col"), None, "dev"), P(("col", "row"), None, "dev"))
    return jax.shard_map(
        per_device, mesh=mesh, in_specs=placed, out_specs=P("row", "col"), check_vma=False
    )
```

profile of v0, /device:TPU:56, one launch (start us, length us, event | category | flops | bytes accessed | tf_op | source)
XLA Modules:
  0.0 398.3 jit_solution(3391028884361926221)
XLA Ops:
  6.5 0.0 all-gather.5.cloned.1.call-start
  6.5 3.4 copy.4
  10.0 0.0 all-gather.5.cloned.1.call-update
  10.0 0.0 all-gather.3.cloned.1.call-start
  10.1 2.8 copy.3
  12.8 0.0 all-gather.3.cloned.1.call-update
  12.9 0.0 all-reduce.3.cloned.1.call-start
  12.9 122.7 %all-gather.5.cloned.1.call-done = bf16[96,2,16384]{2,0,1:T(8,128)(2,1)} async-done(((bf16[24,2,16384]{2,0,1:T(8,128)(2,1)}), bf16[96,2,16384]{2,0,1:T(8,128)(2,1)}) %all-gather.5.cloned.1.call-update) | async-done | bytes 6291472 | tf_op jit(solution)/shard_map/all_gather | solution.py:19
  135.6 4.7 %fusion.1 = f32[96]{0:T(128)} fusion(bf16[96,2,16384]{2,0,1:T(8,128)(2,1)} %all-gather.5.cloned.1.call-done), kind=kLoop, calls=%fused_computation.3 | loop fusion | flops 9437088 | bytes 6291840 | tf_op jit(solution)/shard_map/bpl,bpl->b/dot_general | solution.py:15
  140.3 52.4 %all-gather.3.cloned.1.call-done = bf16[128,2,16384]{2,0,1:T(8,128)(2,1)} async-done(((bf16[16,2,16384]{2,0,1:T(8,128)(2,1)}), bf16[128,2,16384]{2,0,1:T(8,128)(2,1)}) %all-gather.3.cloned.1.call-update) | async-done | bytes 8388624 | tf_op jit(solution)/shard_map/all_gather | solution.py:20
  192.7 0.0 copy-start
  192.7 7.8 %fusion.2 = f32[128,2,96,2]{0,2,3,1:T(8,128)S(1)} fusion(bf16[128,2,16384]{2,0,1:T(8,128)(2,1)} %all-gather.3.cloned.1.call-done, bf16[96,2,16384]{2,0,1:T(8,128)(2,1)} %all-gather.5.cloned.1.call-done), kind=kOutput, calls=%fused_computation.4 | convolution fusion | flops 1610612736 | bytes 14876672 | tf_op jit(solution)/shard_map/bpl,cql->bpcq/dot_general | solution.py:10
  200.5 0.6 fusion.6
  201.1 0.0 copy-done
  201.1 2.3 fusion
  203.4 0.0 all-reduce.3.cloned.1.call-update
  203.4 186.8 %all-reduce.3.cloned.1.call-done = (f32[128,96]{0,1:T(8,128)}, f32[128,96]{0,1:T(8,128)}, f32[96]{0:T(128)}, f32[128]{0:T(128)}) async-done(((f32[128,96]{0,1:T(8,128)}, f32[128,96]{0,1:T(8,128)}, f32[96]{0:T(128)}, f32[128]{0:T(128)}), (f32[128,96]{0,1:T(8,128)}, f32[128,96]{0,1:T(8,128)}, f32[96]{0:T(128)}, f32[128]{0:T(128)})) %all-reduce.3.cloned.1.call-update) | async-done | bytes 99216 | tf_op jit(solution)/shard_map/psum | solution.py:27
  390.2 1.5 multiply_divide_fusion
Async XLA Ops:
  6.5 129.1 %all-gather.5.cloned.1.call-start = ((), (), s32[]{:S(2)}) async-start(), calls=%async_computation.1 | async-start | bytes 7864320 | tf_op jit(solution)/shard_map/all_gather | solution.py:19
  10.0 182.7 %all-gather.3.cloned.1.call-start = ((), (), s32[]{:S(2)}) async-start(), calls=%async_computation | async-start | bytes 9437184 | tf_op jit(solution)/shard_map/all_gather | solution.py:20
  12.9 377.4 %all-reduce.3.cloned.1.call-start = ((), (), s32[]{:S(2)}) async-start(), calls=%async_computation.2 | async-start | bytes 198656 | tf_op jit(solution)/shard_map/psum | solution.py:27
  192.7 8.4 %copy-start = (bf16[128,2,16384]{2,0,1:T(8,128)(2,1)S(1)}, bf16[128,2,16384]{2,0,1:T(8,128)(2,1)}, u32[]{:S(2)}) copy-start(bf16[128,2,16384]{2,0,1:T(8,128)(2,1)} %all-gather.3.cloned.1.call-done) | copy-start | bytes 25165828
Sparse Core Ops, SparseCore 0:
  10.1 125.4 all-gather.4
  137.7 54.9 all-gather.2
  203.5 186.6 all-reduce.2
where the time goes:
time: 399 us; the launch traced here: 398 us
  waiting for transfers between devices  362 us (91%)
  between operations  13.1 us (3%)
  other arithmetic  9.14 us (2%)
  matrix products  7.79 us (2%)
  local copies, waits for them, and re-layouts  6.24 us (2%)
    psum x1, waiting for transfers between devices, per_device(): lax.psum((real_part, imag_part, train_norm, test_norm), 'dev')  187 us
    all_gather x1, waiting for transfers between devices, per_device(): test_panel = lax.all_gather(test_states, 'row', axis=0, tiled=True)  123 us
    all_gather x1, waiting for transfers between devices, per_device(): piece = lax.all_gather(train_states, 'col', axis=0, tiled=True)  52.4 us
  transfers between devices with their start and end apart: 3, of which 3 were waited for; matrix products, arithmetic and copies ran while one was open for 2% of the time, Pallas kernels for 0%

commit v1 on v0

v1 whole, which is shorter than its diff:
```python
import functools

import jax
import jax.numpy as jnp
from jax import lax
from jax.experimental import pallas as pl
from jax.experimental.pallas import tpu as pltpu
from jax.sharding import Mesh, PartitionSpec as P

AMPS = 262144
F32 = jnp.float32
DEV = ("zhi", "y")
SPARE = 192
WINDOW = 63

PLUS = [(i, (i + 1) % 4) for i in range(4)]
MINUS = [(i, (i - 1) % 4) for i in range(4)]
SWAP = [(0, 1), (1, 0)]


def params():
    return pltpu.CompilerParams(vmem_limit_bytes=48 * 1024 * 1024)


def whole(n):
    return [pl.BlockSpec(memory_space=pltpu.VMEM)] * n


def spread(states):
    count = states.shape[0]
    cut = states.reshape(count, 2, 4, 4096).transpose(2, 1, 0, 3)
    return cut


def gather_x(own):
    left = lax.ppermute(own, "x", PLUS)
    right = lax.ppermute(own, "x", MINUS)
    far_a = lax.ppermute(left[:2], "x", PLUS)
    far_b = lax.ppermute(right[2:], "x", MINUS)
    blocks = [own, left, right, far_a, far_b]
    return blocks + [lax.ppermute(b, "core", SWAP) for b in blocks]


def rows_of(refs, lanes):
    out = []
    for core in (0, 5):
        for k in (0, 1, 2):
            r = refs[core + k]
            out.append(r[:, :, lanes].reshape(64, -1))
        a, b = refs[core + 3], refs[core + 4]
        out.append(a[:, :, lanes].reshape(32, -1))
        out.append(b[:, :, lanes].reshape(32, -1))
    return jnp.concatenate(out, axis=0)


def norm_kernel(*refs):
    u, v, out = refs[:10], refs[10:20], refs[20]
    total = jnp.zeros((512, 128), F32)
    for k in range(32):
        for part in (u, v):
            x = rows_of(part, pl.ds(128 * k, 128)).astype(F32)
            total = total + x * x
    sums = jnp.sum(total, axis=1, keepdims=True)
    lane = lax.broadcasted_iota(jnp.int32, (512, 128), 1)
    out[...] = jnp.where(lane == SPARE - 128, sums, 0.0)


def product_kernel(*refs):
    u, v, s_ref, norms, out = refs[:10], refs[10:20], refs[20], refs[21], refs[22]
    nt = (((1,), (1,)), ((), ()))
    width = 512
    gu = jnp.zeros((512, 192), F32)
    gv = jnp.zeros((512, 192), F32)
    ss = jnp.zeros((192, 192), F32)
    for k in range(4096 // width):
        lanes = pl.ds(width * k, width)
        s = s_ref[:, :, lanes].reshape(192, width)
        gu = gu + lax.dot_general(rows_of(u, lanes), s, nt, preferred_element_type=F32)
        gv = gv + lax.dot_general(rows_of(v, lanes), s, nt, preferred_element_type=F32)
        ss = ss + lax.dot_general(s, s, nt, preferred_element_type=F32)

    def pad(x):
        return jnp.concatenate([x, jnp.zeros((x.shape[0], 256 - 192), F32)], axis=1)

    gu, gv, ss = pad(gu), pad(gv), pad(ss)
    lane = lax.broadcasted_iota(jnp.int32, (512, 256), 1)
    first = (lane % 48) < 24
    both = gu + jnp.where(first, pltpu.roll(gv, 256 - 24, 1), -pltpu.roll(gv, 24, 1))
    both = jnp.where(lane < SPARE, both, 0.0)

    r = lax.broadcasted_iota(jnp.int32, (192, 256), 0)
    c = lax.broadcasted_iota(jnp.int32, (192, 256), 1)
    diag = jnp.sum(jnp.where(r == c, ss, 0.0), axis=0, keepdims=True)
    diag = jnp.broadcast_to(diag, (8, 256))
    sub = lax.broadcasted_iota(jnp.int32, (8, 256), 0)
    lane8 = lax.broadcasted_iota(jnp.int32, (8, 256), 1)
    spare = jnp.zeros((8, 256), F32)
    for w in range(4):
        moved = pltpu.roll(diag, (SPARE + 1 - WINDOW * w) % 256, 1)
        keep = (sub == w) & (lane8 > SPARE)
        spare = spare + jnp.where(keep, moved, 0.0)

    tn = jnp.concatenate([jnp.zeros((512, 128), F32), norms[...]], axis=1)
    both = (both + tn).reshape(64, 8, 256) + spare[None]
    both = both.reshape(8, 4, 2, 8, 256)
    for j in range(8):
        out[:, 2 * j : 2 * j + 2] = both[j]


def per_device(train, test):
    t = spread(train)
    s = spread(test).reshape(4, 48, 4096)
    a2a = functools.partial(lax.all_to_all, split_axis=0, concat_axis=0, tiled=True)
    u = a2a(t[:, 0], "row")
    v_in, u = lax.optimization_barrier((t[:, 1], u))
    v = a2a(v_in, "row")
    s_in, v = lax.optimization_barrier((s, v))
    s = a2a(s_in, "row")
    us, vs = gather_x(u), gather_x(v)
    norms = pl.pallas_call(
        norm_kernel,
        out_shape=jax.ShapeDtypeStruct((512, 128), F32),
        in_specs=whole(20),
        out_specs=pl.BlockSpec(memory_space=pltpu.VMEM),
        compiler_params=params(),
        name="norms",
    )(*us, *vs)
    pieces = pl.pallas_call(
        product_kernel,
        out_shape=jax.ShapeDtypeStruct((4, 16, 8, 256), F32),
        in_specs=whole(22),
        out_specs=pl.BlockSpec(memory_space=pltpu.VMEM),
        compiler_params=params(),
        name="products",
    )(*us, *vs, s, norms)
    parts = a2a(pieces.reshape(64, 8, 256), ("row",) + DEV)
    total = jnp.sum(parts, axis=0)
    g = total[:, :SPARE].reshape(8, 4, 2, 24)
    power = (g[:, :, 0] ** 2 + g[:, :, 1] ** 2).reshape(8, 96)
    tn = total[:, SPARE : SPARE + 1]
    diag = total[:4, SPARE + 1 :].reshape(4 * WINDOW)[:192].reshape(4, 2, 24)
    sn = (diag[:, 0] + diag[:, 1]).reshape(1, 96)
    block = float(AMPS) * power / (tn * sn)
    full = a2a(jnp.broadcast_to(block[None], (16, 8, 96)), DEV)
    full = full.reshape(2, 4, 16, 96)
    core, x = lax.axis_index("core"), lax.axis_index("x")
    full = jnp.where(core == 0, full, full[::-1])
    full = full[:, jnp.array([0, 2, 3, 1])]
    full = full.transpose(1, 0, 2, 3)
    full = lax.dynamic_slice_in_dim(jnp.concatenate([full, full]), (4 - x) % 4, 4, 0)
    return full.reshape(128, 96)


def solution(mesh):
    axes = ("row", "x", "core", "zhi", "y")
    fine = Mesh(mesh.devices.reshape(4, 4, 2, 2, 8), axes)
    placed = (
        P(("row", "x", "core"), None, DEV),
        P(("x", "core", "row"), None, DEV),
    )
    return jax.shard_map(
        per_device, mesh=fine, in_specs=placed, out_specs=P("row", ("x", "core")), check_vma=False
    )
```

time: 399 us -> 193 us (0.48)
  the two profiles are of different devices: /device:TPU:56 before, /device:TPU:8 now
where the time goes in v1:
time: 193 us; the launch traced here: 192 us
  starting transfers between devices  75.5 us (39%)
  waiting for transfers between devices  57.4 us (30%)
  local copies, waits for them, and re-layouts  27.4 us (14%)
  blocking collectives  21.5 us (11%)
  Pallas kernels  8.87 us (5%)
    all_to_all x1, blocking collectives, per_device(): u = a2a(t[:, 0], 'row')  21.5 us
    ppermute x10, starting transfers between devices, gather_x(): return blocks + [lax.ppermute(b, 'core', SWAP) for b in blocks]  20.6 us
    all_to_all x1, waiting for transfers between devices, per_device(): parts = a2a(pieces.reshape(64, 8, 256), ('row',) + DEV)  18.5 us
    unnamed x52, local copies, waits for them, and re-layouts  16.8 us
    all_to_all x1, starting transfers between devices, per_device(): parts = a2a(pieces.reshape(64, 8, 256), ('row',) + DEV)  14 us
    all_to_all x1, waiting for transfers between devices, per_device(): full = a2a(jnp.broadcast_to(block[None], (16, 8, 96)), DEV)  11.4 us
    ppermute x2, starting transfers between devices, gather_x(): right = lax.ppermute(own, 'x', MINUS)  9.8 us
    all_to_all x1, waiting for transfers between devices, per_device(): v = a2a(v_in, 'row')  8.8 us
  transfers between devices with their start and end apart: 22, of which 8 were waited for; matrix products, arithmetic and copies ran while one was open for 3% of the time, Pallas kernels for 2%

profile of v1, /device:TPU:8, one launch (start us, length us, event | category | flops | bytes accessed | tf_op | source)
XLA Modules:
  0.0 191.5 jit_solution(9842520511592563093)
XLA Ops:
  3.2 21.5 %all_to_all.25.refs_0_ = bf16[4,16,4096]{2,1,0:T(8,128)(2,1)S(1)} all-to-all(bf16[4,16,4096]{2,1,0:T(8,128)(2,1)S(1)} %get-tuple-element.13), channel_id=1, replica_groups=mesh['row'=4,'x'=4,'core'=2,'zhi'=2,'y'=8] {'row'}, dimensions={0} | all-to-all | bytes 1048576 | tf_op jit(solution)/shard_map/all_to_all | solution.py:114
  24.7 3.5 %all-to-all-start.1 = ((bf16[4,16,4096]{2,1,0:T(8,128)(2,1)}), bf16[4,16,4096]{2,1,0:T(8,128)(2,1)S(1)}, u32[]{:S(2)}, u32[]{:S(2)}) async-start(bf16[4,16,4096]{2,1,0:T(8,128)(2,1)} %get-tuple-element.10), calls=%async_computation.1 | async-start | bytes 1048576 | tf_op jit(solution)/shard_map/all_to_all | solution.py:116
  28.2 2.8 %reshape.88 = bf16[24,2,4,4096]{3,2,1,0:T(4,128)(2,1)S(1)} reshape(bf16[24,2,16384]{2,1,0:T(2,128)(2,1)} %param.4) | data formatting | bytes 3145728 | tf_op jit(solution)/shard_map/reshape | solution.py:31
  31.0 2.0 %copy.12 = bf16[24,2,4,4096]{3,0,1,2:T(8,128)(2,1)} copy(bf16[24,2,4,4096]{3,2,1,0:T(4,128)(2,1)S(1)} %reshape.88) | data formatting | bytes 3145728 | tf_op jit(solution)/shard_map/reshape | solution.py:31
  33.0 8.8 %all-to-all-done.1.refs_10_ = bf16[4,16,4096]{2,1,0:T(8,128)(2,1)S(1)} async-done(((bf16[4,16,4096]{2,1,0:T(8,128)(2,1)}), bf16[4,16,4096]{2,1,0:T(8,128)(2,1)S(1)}, u32[]{:S(2)}, u32[]{:S(2)}) %all-to-all-start.1) | async-done | bytes 524320 | tf_op jit(solution)/shard_map/all_to_all | solution.py:116
  41.8 4.3 %all-to-all-start.2 = ((bf16[4,48,4096]{2,1,0:T(8,128)(2,1)}), bf16[4,48,4096]{2,1,0:T(8,128)(2,1)}, u32[]{:S(2)}, u32[]{:S(2)}) async-start(bf16[4,48,4096]{2,1,0:T(8,128)(2,1)} %bitcast.4), calls=%async_computation.2 | async-start | bytes 3145728 | tf_op jit(solution)/shard_map/all_to_all | solution.py:118
  46.2 4.7 %collective-permute-start.1 = (bf16[4,16,4096]{2,1,0:T(8,128)(2,1)S(1)}, bf16[4,16,4096]{2,1,0:T(8,128)(2,1)S(1)}, u32[]{:S(2)}, u32[]{:S(2)}) collective-permute-start(bf16[4,16,4096]{2,1,0:T(8,128)(2,1)S(1)} %all_to_all.25.refs_0_), channel_id=1, source_target_pairs={{0,96},{32,0},{64,32},{96,64},{1,97},{33,1},{65,33},{97,65},{2,98}... | collective-permute-start | bytes 1572872 | tf_op jit(solution)/shard_map/ppermute | solution.py:37
  50.8 1.9 %collective-permute-start = (bf16[4,16,4096]{2,1,0:T(8,128)(2,1)S(1)}, bf16[4,16,4096]{2,1,0:T(8,128)(2,1)S(1)}, u32[]{:S(2)}, u32[]{:S(2)}) collective-permute-start(bf16[4,16,4096]{2,1,0:T(8,128)(2,1)S(1)} %all_to_all.25.refs_0_), channel_id=1, source_target_pairs={{0,32},{32,64},{64,96},{96,0},{1,33},{33,65},{65,97},{97,1},{2,34}... | collective-permute-start | bytes 1572872 | tf_op jit(solution)/shard_map/ppermute | solution.py:36
  52.8 5.1 %collective-permute-start.10 = (bf16[4,16,4096]{2,1,0:T(8,128)(2,1)S(1)}, bf16[4,16,4096]{2,1,0:T(8,128)(2,1)S(1)}, u32[]{:S(2)}, u32[]{:S(2)}) collective-permute-start(bf16[4,16,4096]{2,1,0:T(8,128)(2,1)S(1)} %all-to-all-done.1.refs_10_), channel_id=1, source_target_pairs={{0,96},{32,0},{64,32},{96,64},{1,97},{33,1},{65,33},{97,65},{2,98}... | collective-permute-start | bytes 1572872 | tf_op jit(solution)/shard_map/ppermute | solution.py:37
  57.9 5.3 %collective-permute-done.1.refs_2_ = bf16[4,16,4096]{2,1,0:T(8,128)(2,1)S(1)} collective-permute-done((bf16[4,16,4096]{2,1,0:T(8,128)(2,1)S(1)}, bf16[4,16,4096]{2,1,0:T(8,128)(2,1)S(1)}, u32[]{:S(2)}, u32[]{:S(2)}) %collective-permute-start.1) | collective-permute-done | bytes 524320 | tf_op jit(solution)/shard_map/ppermute | solution.py:37
  63.2 5.6 %collective-permute-start.3 = (bf16[2,16,4096]{2,1,0:T(8,128)(2,1)S(1)}, bf16[2,16,4096]{2,1,0:T(8,128)(2,1)S(1)}, u32[]{:S(2)}, u32[]{:S(2)}) collective-permute-start(bf16[2,16,4096]{2,1,0:T(8,128)(2,1)S(1)} %slice.61), channel_id=1, source_target_pairs={{0,96},{32,0},{64,32},{96,64},{1,97},{33,1},{65,33},{97,65},{2,98}... | collective-permute-start | bytes 786440 | tf_op jit(solution)/shard_map/ppermute | solution.py:39
  74.6 3.4 %collective-permute-done.3.refs_4_ = bf16[2,16,4096]{2,1,0:T(8,128)(2,1)S(1)} collective-permute-done((bf16[2,16,4096]{2,1,0:T(8,128)(2,1)S(1)}, bf16[2,16,4096]{2,1,0:T(8,128)(2,1)S(1)}, u32[]{:S(2)}, u32[]{:S(2)}) %collective-permute-start.3) | collective-permute-done | bytes 262176 | tf_op jit(solution)/shard_map/ppermute | solution.py:39
  80.0 7.4 %collective-permute-done.2.refs_3_ = bf16[2,16,4096]{2,1,0:T(8,128)(2,1)S(1)} collective-permute-done((bf16[2,16,4096]{2,1,0:T(8,128)(2,1)S(1)}, bf16[2,16,4096]{2,1,0:T(8,128)(2,1)S(1)}, u32[]{:S(2)}, u32[]{:S(2)}) %collective-permute-start.2) | collective-permute-done | bytes 262176 | tf_op jit(solution)/shard_map/ppermute | solution.py:38
  89.3 2.4 %collective-permute-start.8 = (bf16[2,16,4096]{2,1,0:T(8,128)(2,1)S(1)}, bf16[2,16,4096]{2,1,0:T(8,128)(2,1)S(1)}, u32[]{:S(2)}, u32[]{:S(2)}) collective-permute-start(bf16[2,16,4096]{2,1,0:T(8,128)(2,1)S(1)} %collective-permute-done.3.refs_4_), channel_id=1, source_target_pairs={{0,16},{16,0},{1,17},{17,1},{2,18},{18,2},{3,19},{19,3},{4,20},{20... | collective-permute-start | bytes 786440 | tf_op jit(solution)/shard_map/ppermute | solution.py:41
  91.7 1.9 %collective-permute-start.7 = (bf16[2,16,4096]{2,1,0:T(8,128)(2,1)S(1)}, bf16[2,16,4096]{2,1,0:T(8,128)(2,1)S(1)}, u32[]{:S(2)}, u32[]{:S(2)}) collective-permute-start(bf16[2,16,4096]{2,1,0:T(8,128)(2,1)S(1)} %collective-permute-done.2.refs_3_), channel_id=1, source_target_pairs={{0,16},{16,0},{1,17},{17,1},{2,18},{18,2},{3,19},{19,3},{4,20},{20... | collective-permute-start | bytes 786440 | tf_op jit(solution)/shard_map/ppermute | solution.py:41
  93.7 2.4 %collective-permute-start.13 = (bf16[4,16,4096]{2,1,0:T(8,128)(2,1)S(1)}, bf16[4,16,4096]{2,1,0:T(8,128)(2,1)S(1)}, u32[]{:S(2)}, u32[]{:S(2)}) collective-permute-start(bf16[4,16,4096]{2,1,0:T(8,128)(2,1)S(1)} %all-to-all-done.1.refs_10_), channel_id=1, source_target_pairs={{0,16},{16,0},{1,17},{17,1},{2,18},{18,2},{3,19},{19,3},{4,20},{20... | collective-permute-start | bytes 1572872 | tf_op jit(solution)/shard_map/ppermute | solution.py:41
  98.1 3.9 %collective-permute-start.11 = (bf16[2,16,4096]{2,1,0:T(8,128)(2,1)S(1)}, bf16[2,16,4096]{2,1,0:T(8,128)(2,1)S(1)}, u32[]{:S(2)}, u32[]{:S(2)}) collective-permute-start(bf16[2,16,4096]{2,1,0:T(8,128)(2,1)S(1)} %slice.62), channel_id=1, source_target_pairs={{0,32},{32,64},{64,96},{96,0},{1,33},{33,65},{65,97},{97,1},{2,34}... | collective-permute-start | bytes 786440 | tf_op jit(solution)/shard_map/ppermute | solution.py:38
  104.0 2.4 %collective-permute-start.14 = (bf16[4,16,4096]{2,1,0:T(8,128)(2,1)S(1)}, bf16[4,16,4096]{2,1,0:T(8,128)(2,1)S(1)}, u32[]{:S(2)}, u32[]{:S(2)}) collective-permute-start(bf16[4,16,4096]{2,1,0:T(8,128)(2,1)S(1)} %collective-permute-done.9.refs_11_), channel_id=1, source_target_pairs={{0,16},{16,0},{1,17},{17,1},{2,18},{18,2},{3,19},{19,3},{4,20},{20... | collective-permute-start | bytes 1572872 | tf_op jit(solution)/shard_map/ppermute | solution.py:41
  114.4 3.5 %norms.1.refs_21_ = f32[512,128]{1,0:T(8,128)S(1)} custom-call(bf16[4,16,4096]{2,1,0:T(8,128)(2,1)S(1)} %all_to_all.25.refs_0_, bf16[4,16,4096]{2,1,0:T(8,128)(2,1)S(1)} %collective-permute-done.refs_1_, bf16[4,16,4096]{2,1,0:T(8,128)(2,1)S(1)} %collective-permute-done.1.refs_2_, bf16[2,16,4096]{2,1,0:T(8,128)(2,1)S(1)} %collective-permute-done.2.refs_3_, ...), custom_call_target="tpu_custom_call" | custom-call | tf_op jit(solution)/shard_map/norms/pallas_call | solution.py:120
  132.4 5.4 %products.1 = f32[4,16,8,256]{3,2,1,0:T(8,128)S(1)} custom-call(bf16[4,16,4096]{2,1,0:T(8,128)(2,1)S(1)} %all_to_all.25.refs_0_, bf16[4,16,4096]{2,1,0:T(8,128)(2,1)S(1)} %collective-permute-done.refs_1_, bf16[4,16,4096]{2,1,0:T(8,128)(2,1)S(1)} %collective-permute-done.1.refs_2_, bf16[2,16,4096]{2,1,0:T(8,128)(2,1)S(1)} %copy-done.5, ...), custom_call_target="tpu_custom_call" | custom-call | tf_op jit(solution)/shard_map/products/pallas_call | solution.py:128
  138.5 14.0 %all-to-all-start.3 = ((f32[64,8,256]{2,1,0:T(8,128)}), f32[64,8,256]{2,1,0:T(8,128)S(1)}, u32[]{:S(2)}, u32[]{:S(2)}) async-start(f32[64,8,256]{2,1,0:T(8,128)} %bitcast.15), calls=%async_computation.3 | async-start | bytes 1048576 | tf_op jit(solution)/shard_map/all_to_all | solution.py:136
  152.6 18.5 %all-to-all-done.3 = f32[64,8,256]{2,1,0:T(8,128)S(1)} async-done(((f32[64,8,256]{2,1,0:T(8,128)}), f32[64,8,256]{2,1,0:T(8,128)S(1)}, u32[]{:S(2)}, u32[]{:S(2)}) %all-to-all-start.3) | async-done | bytes 524320 | tf_op jit(solution)/shard_map/all_to_all | solution.py:136
  172.7 6.1 %all-to-all-start.4 = ((f32[16,8,96]{2,1,0:T(8,128)}), f32[16,8,96]{2,1,0:T(8,128)S(1)}, u32[]{:S(2)}, u32[]{:S(2)}) async-start(f32[16,8,96]{2,1,0:T(8,128)} %broadcast_in_dim.4), calls=%async_computation.4 | async-start | bytes 131072 | tf_op jit(solution)/shard_map/all_to_all | solution.py:144
  178.8 11.4 %all-to-all-done.4 = f32[16,8,96]{2,1,0:T(8,128)S(1)} async-done(((f32[16,8,96]{2,1,0:T(8,128)}), f32[16,8,96]{2,1,0:T(8,128)S(1)}, u32[]{:S(2)}, u32[]{:S(2)}) %all-to-all-start.4) | async-done | bytes 49184 | tf_op jit(solution)/shard_map/all_to_all | solution.py:144
  (101 shorter events, 42.8 us)
Async XLA Ops:
  24.7 17.1 %all-to-all-start.1 = ((bf16[4,16,4096]{2,1,0:T(8,128)(2,1)}), bf16[4,16,4096]{2,1,0:T(8,128)(2,1)S(1)}, u32[]{:S(2)}, u32[]{:S(2)}) async-start(bf16[4,16,4096]{2,1,0:T(8,128)(2,1)} %get-tuple-element.10), calls=%async_computation.1 | async-start | bytes 1048576 | tf_op jit(solution)/shard_map/all_to_all | solution.py:116
  41.8 71.0 %copy-start = (bf16[4,16,4096]{2,1,0:T(8,128)(2,1)}, bf16[4,16,4096]{2,1,0:T(8,128)(2,1)S(1)}, u32[]{:S(2)}) copy-start(bf16[4,16,4096]{2,1,0:T(8,128)(2,1)S(1)} %all-to-all-done.1.refs_10_) | copy-start | bytes 1572868
  41.8 81.9 %all-to-all-start.2 = ((bf16[4,48,4096]{2,1,0:T(8,128)(2,1)}), bf16[4,48,4096]{2,1,0:T(8,128)(2,1)}, u32[]{:S(2)}, u32[]{:S(2)}) async-start(bf16[4,48,4096]{2,1,0:T(8,128)(2,1)} %bitcast.4), calls=%async_computation.2 | async-start | bytes 3145728 | tf_op jit(solution)/shard_map/all_to_all | solution.py:118
  46.2 17.0 %collective-permute-start.1 = (bf16[4,16,4096]{2,1,0:T(8,128)(2,1)S(1)}, bf16[4,16,4096]{2,1,0:T(8,128)(2,1)S(1)}, u32[]{:S(2)}, u32[]{:S(2)}) collective-permute-start(bf16[4,16,4096]{2,1,0:T(8,128)(2,1)S(1)} %all_to_all.25.refs_0_), channel_id=1, source_target_pairs={{0,96},{32,0},{64,32},{96,64},{1,97},{33,1},{65,33},{97,65},{2,98}... | collective-permute-start | bytes 1572872 | tf_op jit(solution)/shard_map/ppermute | solution.py:37
  50.8 19.9 %collective-permute-start = (bf16[4,16,4096]{2,1,0:T(8,128)(2,1)S(1)}, bf16[4,16,4096]{2,1,0:T(8,128)(2,1)S(1)}, u32[]{:S(2)}, u32[]{:S(2)}) collective-permute-start(bf16[4,16,4096]{2,1,0:T(8,128)(2,1)S(1)} %all_to_all.25.refs_0_), channel_id=1, source_target_pairs={{0,32},{32,64},{64,96},{96,0},{1,33},{33,65},{65,97},{97,1},{2,34}... | collective-permute-start | bytes 1572872 | tf_op jit(solution)/shard_map/ppermute | solution.py:36
  52.8 36.5 %collective-permute-start.10 = (bf16[4,16,4096]{2,1,0:T(8,128)(2,1)S(1)}, bf16[4,16,4096]{2,1,0:T(8,128)(2,1)S(1)}, u32[]{:S(2)}, u32[]{:S(2)}) collective-permute-start(bf16[4,16,4096]{2,1,0:T(8,128)(2,1)S(1)} %all-to-all-done.1.refs_10_), channel_id=1, source_target_pairs={{0,96},{32,0},{64,32},{96,64},{1,97},{33,1},{65,33},{97,65},{2,98}... | collective-permute-start | bytes 1572872 | tf_op jit(solution)/shard_map/ppermute | solution.py:37
  63.2 14.8 %collective-permute-start.3 = (bf16[2,16,4096]{2,1,0:T(8,128)(2,1)S(1)}, bf16[2,16,4096]{2,1,0:T(8,128)(2,1)S(1)}, u32[]{:S(2)}, u32[]{:S(2)}) collective-permute-start(bf16[2,16,4096]{2,1,0:T(8,128)(2,1)S(1)} %slice.61), channel_id=1, source_target_pairs={{0,96},{32,0},{64,32},{96,64},{1,97},{33,1},{65,33},{97,65},{2,98}... | collective-permute-start | bytes 786440 | tf_op jit(solution)/shard_map/ppermute | solution.py:39
  68.8 22.9 %collective-permute-start.9 = (bf16[4,16,4096]{2,1,0:T(8,128)(2,1)S(1)}, bf16[4,16,4096]{2,1,0:T(8,128)(2,1)S(1)}, u32[]{:S(2)}, u32[]{:S(2)}) collective-permute-start(bf16[4,16,4096]{2,1,0:T(8,128)(2,1)S(1)} %all-to-all-done.1.refs_10_), channel_id=1, source_target_pairs={{0,32},{32,64},{64,96},{96,0},{1,33},{33,65},{65,97},{97,1},{2,34}... | collective-permute-start | bytes 1572872 | tf_op jit(solution)/shard_map/ppermute | solution.py:36
  70.8 16.5 %collective-permute-start.2 = (bf16[2,16,4096]{2,1,0:T(8,128)(2,1)S(1)}, bf16[2,16,4096]{2,1,0:T(8,128)(2,1)S(1)}, u32[]{:S(2)}, u32[]{:S(2)}) collective-permute-start(bf16[2,16,4096]{2,1,0:T(8,128)(2,1)S(1)} %slice.60), channel_id=1, source_target_pairs={{0,32},{32,64},{64,96},{96,0},{1,33},{33,65},{65,97},{97,1},{2,34}... | collective-permute-start | bytes 786440 | tf_op jit(solution)/shard_map/ppermute | solution.py:38
  72.7 21.0 %collective-permute-start.4 = (bf16[4,16,4096]{2,1,0:T(8,128)(2,1)S(1)}, bf16[4,16,4096]{2,1,0:T(8,128)(2,1)S(1)}, u32[]{:S(2)}, u32[]{:S(2)}) collective-permute-start(bf16[4,16,4096]{2,1,0:T(8,128)(2,1)S(1)} %all_to_all.25.refs_0_), channel_id=1, source_target_pairs={{0,16},{16,0},{1,17},{17,1},{2,18},{18,2},{3,19},{19,3},{4,20},{20... | collective-permute-start | bytes 1572872 | tf_op jit(solution)/shard_map/ppermute | solution.py:41
  78.1 20.0 %collective-permute-start.6 = (bf16[4,16,4096]{2,1,0:T(8,128)(2,1)S(1)}, bf16[4,16,4096]{2,1,0:T(8,128)(2,1)S(1)}, u32[]{:S(2)}, u32[]{:S(2)}) collective-permute-start(bf16[4,16,4096]{2,1,0:T(8,128)(2,1)S(1)} %collective-permute-done.1.refs_2_), channel_id=1, source_target_pairs={{0,16},{16,0},{1,17},{17,1},{2,18},{18,2},{3,19},{19,3},{4,20},{20... | collective-permute-start | bytes 1572872 | tf_op jit(solution)/shard_map/ppermute | solution.py:41
  87.3 16.6 %collective-permute-start.5 = (bf16[4,16,4096]{2,1,0:T(8,128)(2,1)S(1)}, bf16[4,16,4096]{2,1,0:T(8,128)(2,1)S(1)}, u32[]{:S(2)}, u32[]{:S(2)}) collective-permute-start(bf16[4,16,4096]{2,1,0:T(8,128)(2,1)S(1)} %collective-permute-done.refs_1_), channel_id=1, source_target_pairs={{0,16},{16,0},{1,17},{17,1},{2,18},{18,2},{3,19},{19,3},{4,20},{20... | collective-permute-start | bytes 1572872 | tf_op jit(solution)/shard_map/ppermute | solution.py:41
  89.3 6.8 %collective-permute-start.8 = (bf16[2,16,4096]{2,1,0:T(8,128)(2,1)S(1)}, bf16[2,16,4096]{2,1,0:T(8,128)(2,1)S(1)}, u32[]{:S(2)}, u32[]{:S(2)}) collective-permute-start(bf16[2,16,4096]{2,1,0:T(8,128)(2,1)S(1)} %collective-permute-done.3.refs_4_), channel_id=1, source_target_pairs={{0,16},{16,0},{1,17},{17,1},{2,18},{18,2},{3,19},{19,3},{4,20},{20... | collective-permute-start | bytes 786440 | tf_op jit(solution)/shard_map/ppermute | solution.py:41
  91.7 10.3 %collective-permute-start.7 = (bf16[2,16,4096]{2,1,0:T(8,128)(2,1)S(1)}, bf16[2,16,4096]{2,1,0:T(8,128)(2,1)S(1)}, u32[]{:S(2)}, u32[]{:S(2)}) collective-permute-start(bf16[2,16,4096]{2,1,0:T(8,128)(2,1)S(1)} %collective-permute-done.2.refs_3_), channel_id=1, source_target_pairs={{0,16},{16,0},{1,17},{17,1},{2,18},{18,2},{3,19},{19,3},{4,20},{20... | collective-permute-start | bytes 786440 | tf_op jit(solution)/shard_map/ppermute | solution.py:41
  93.7 17.6 %collective-permute-start.13 = (bf16[4,16,4096]{2,1,0:T(8,128)(2,1)S(1)}, bf16[4,16,4096]{2,1,0:T(8,128)(2,1)S(1)}, u32[]{:S(2)}, u32[]{:S(2)}) collective-permute-start(bf16[4,16,4096]{2,1,0:T(8,128)(2,1)S(1)} %all-to-all-done.1.refs_10_), channel_id=1, source_target_pairs={{0,16},{16,0},{1,17},{17,1},{2,18},{18,2},{3,19},{19,3},{4,20},{20... | collective-permute-start | bytes 1572872 | tf_op jit(solution)/shard_map/ppermute | solution.py:41
  96.1 10.2 %collective-permute-start.12 = (bf16[2,16,4096]{2,1,0:T(8,128)(2,1)S(1)}, bf16[2,16,4096]{2,1,0:T(8,128)(2,1)S(1)}, u32[]{:S(2)}, u32[]{:S(2)}) collective-permute-start(bf16[2,16,4096]{2,1,0:T(8,128)(2,1)S(1)} %slice.63), channel_id=1, source_target_pairs={{0,96},{32,0},{64,32},{96,64},{1,97},{33,1},{65,33},{97,65},{2,98}... | collective-permute-start | bytes 786440 | tf_op jit(solution)/shard_map/ppermute | solution.py:39
  98.1 11.3 %collective-permute-start.11 = (bf16[2,16,4096]{2,1,0:T(8,128)(2,1)S(1)}, bf16[2,16,4096]{2,1,0:T(8,128)(2,1)S(1)}, u32[]{:S(2)}, u32[]{:S(2)}) collective-permute-start(bf16[2,16,4096]{2,1,0:T(8,128)(2,1)S(1)} %slice.62), channel_id=1, source_target_pairs={{0,32},{32,64},{64,96},{96,0},{1,33},{33,65},{65,97},{97,1},{2,34}... | collective-permute-start | bytes 786440 | tf_op jit(solution)/shard_map/ppermute | solution.py:38
  102.0 10.8 %collective-permute-start.15 = (bf16[4,16,4096]{2,1,0:T(8,128)(2,1)S(1)}, bf16[4,16,4096]{2,1,0:T(8,128)(2,1)S(1)}, u32[]{:S(2)}, u32[]{:S(2)}) collective-permute-start(bf16[4,16,4096]{2,1,0:T(8,128)(2,1)S(1)} %collective-permute-done.10.refs_12_), channel_id=1, source_target_pairs={{0,16},{16,0},{1,17},{17,1},{2,18},{18,2},{3,19},{19,3},{4,20},{20... | collective-permute-start | bytes 1572872 | tf_op jit(solution)/shard_map/ppermute | solution.py:41
  104.0 8.9 %collective-permute-start.14 = (bf16[4,16,4096]{2,1,0:T(8,128)(2,1)S(1)}, bf16[4,16,4096]{2,1,0:T(8,128)(2,1)S(1)}, u32[]{:S(2)}, u32[]{:S(2)}) collective-permute-start(bf16[4,16,4096]{2,1,0:T(8,128)(2,1)S(1)} %collective-permute-done.9.refs_11_), channel_id=1, source_target_pairs={{0,16},{16,0},{1,17},{17,1},{2,18},{18,2},{3,19},{19,3},{4,20},{20... | collective-permute-start | bytes 1572872 | tf_op jit(solution)/shard_map/ppermute | solution.py:41
  106.4 5.0 %collective-permute-start.17 = (bf16[2,16,4096]{2,1,0:T(8,128)(2,1)S(1)}, bf16[2,16,4096]{2,1,0:T(8,128)(2,1)S(1)}, u32[]{:S(2)}, u32[]{:S(2)}) collective-permute-start(bf16[2,16,4096]{2,1,0:T(8,128)(2,1)S(1)} %collective-permute-done.12.refs_14_), channel_id=1, source_target_pairs={{0,16},{16,0},{1,17},{17,1},{2,18},{18,2},{3,19},{19,3},{4,20},{20... | collective-permute-start | bytes 786440 | tf_op jit(solution)/shard_map/ppermute | solution.py:41
  109.4 3.4 %collective-permute-start.16 = (bf16[2,16,4096]{2,1,0:T(8,128)(2,1)S(1)}, bf16[2,16,4096]{2,1,0:T(8,128)(2,1)S(1)}, u32[]{:S(2)}, u32[]{:S(2)}) collective-permute-start(bf16[2,16,4096]{2,1,0:T(8,128)(2,1)S(1)} %collective-permute-done.11.refs_13_), channel_id=1, source_target_pairs={{0,16},{16,0},{1,17},{17,1},{2,18},{18,2},{3,19},{19,3},{4,20},{20... | collective-permute-start | bytes 786440 | tf_op jit(solution)/shard_map/ppermute | solution.py:41
  138.5 40.2 %copy-start.25 = (s32[4]{0:T(128)S(1)}, s32[4]{0:T(128)}, u32[]{:S(2)}) copy-start(s32[4]{0:T(128)} %constant.43) | copy-start | bytes 52
  138.5 32.5 %all-to-all-start.3 = ((f32[64,8,256]{2,1,0:T(8,128)}), f32[64,8,256]{2,1,0:T(8,128)S(1)}, u32[]{:S(2)}, u32[]{:S(2)}) async-start(f32[64,8,256]{2,1,0:T(8,128)} %bitcast.15), calls=%async_computation.3 | async-start | bytes 1048576 | tf_op jit(solution)/shard_map/all_to_all | solution.py:136
  172.7 17.5 %all-to-all-start.4 = ((f32[16,8,96]{2,1,0:T(8,128)}), f32[16,8,96]{2,1,0:T(8,128)S(1)}, u32[]{:S(2)}, u32[]{:S(2)}) async-start(f32[16,8,96]{2,1,0:T(8,128)} %broadcast_in_dim.4), calls=%async_computation.4 | async-start | bytes 131072 | tf_op jit(solution)/shard_map/all_to_all | solution.py:144
  (24 other events, 88.6 us)

commit v2 on v0

v2 whole, which is shorter than its diff:
```python
import functools

import jax
import jax.numpy as jnp
from jax import lax
from jax.experimental import pallas as pl
from jax.experimental.pallas import tpu as pltpu
from jax.sharding import Mesh, PartitionSpec as P

AMPS = 262144
F32 = jnp.float32
DEV = ("zhi", "y")
SPARE = 192
WINDOW = 63

K_STEP = 512
SWAP = [(0, 1), (1, 0)]
AROUND = [(2 * x + c, 2 * ((x + (1, -1)[c]) % 4) + c) for x in range(4) for c in (0, 1)]


def params():
    return pltpu.CompilerParams(vmem_limit_bytes=48 * 1024 * 1024)


def spread(states):
    return states.reshape(states.shape[0], 2, 4, 4096).transpose(2, 1, 0, 3)


def swap(block):
    return lax.ppermute(block, "core", SWAP)


def around(block):
    return lax.ppermute(block, ("x", "core"), AROUND)


def product_kernel(place, *refs):
    u_refs, v_refs, (s_ref, out, gu, gv, ss, tt) = refs[:6], refs[6:12], refs[12:]
    k = pl.program_id(0)
    nt = (((1,), (1,)), ((), ()))

    @pl.when(k == 0)
    def _():
        gu[...] = jnp.zeros_like(gu)
        gv[...] = jnp.zeros_like(gv)
        ss[...] = jnp.zeros_like(ss)
        tt[...] = jnp.zeros_like(tt)

    u = jnp.concatenate([r[...] for r in u_refs], axis=0).reshape(512, K_STEP)
    v = jnp.concatenate([r[...] for r in v_refs], axis=0).reshape(512, K_STEP)
    s = s_ref[...].reshape(192, K_STEP)
    gu[:, :SPARE] += lax.dot_general(u, s, nt, preferred_element_type=F32)
    gv[:, :SPARE] += lax.dot_general(v, s, nt, preferred_element_type=F32)
    ss[:, :SPARE] += lax.dot_general(s, s, nt, preferred_element_type=F32)
    total = tt[...]
    for j in range(K_STEP // 128):
        for part in (u, v):
            x = part[:, 128 * j : 128 * j + 128].astype(F32)
            total = total + x * x
    tt[...] = total

    @pl.when(k == pl.num_programs(0) - 1)
    def _():
        lane = lax.broadcasted_iota(jnp.int32, (512, 256), 1)
        first = (lane % 48) < 24
        g = gv[...]
        both = gu[...] + jnp.where(first, pltpu.roll(g, 256 - 24, 1), -pltpu.roll(g, 24, 1))
        tn = jnp.sum(tt[...], axis=1, keepdims=True)
        both = jnp.where(lane < SPARE, both, jnp.where(lane == SPARE, tn, 0.0))

        r = lax.broadcasted_iota(jnp.int32, (192, 256), 0)
        c = lax.broadcasted_iota(jnp.int32, (192, 256), 1)
        diag = jnp.sum(jnp.where(r == c, ss[...], 0.0), axis=0, keepdims=True)
        diag = jnp.broadcast_to(diag, (8, 256))
        sub = lax.broadcasted_iota(jnp.int32, (8, 256), 0)
        lane8 = lax.broadcasted_iota(jnp.int32, (8, 256), 1)
        spare = jnp.zeros((8, 256), F32)
        for w in range(4):
            moved = pltpu.roll(diag, (SPARE + 1 - WINDOW * w) % 256, 1)
            spare = spare + jnp.where((sub == w) & (lane8 > SPARE), moved, 0.0)

        both = (both.reshape(64, 8, 256) + spare[None]).reshape(8, 4, 2, 8, 256)
        for j in range(8):
            out[:, pl.ds(2 * place[j], 2)] = both[j]


def products(place, u, v, s):
    blocks = [pl.BlockSpec((b.shape[0], 16, K_STEP), lambda k: (0, 0, k)) for b in (*u, *v)]
    return pl.pallas_call(
        product_kernel,
        out_shape=jax.ShapeDtypeStruct((4, 16, 8, 256), F32),
        grid=(4096 // K_STEP,),
        in_specs=[
            pl.BlockSpec(memory_space=pltpu.SMEM),
            *blocks,
            pl.BlockSpec((4, 48, K_STEP), lambda k: (0, 0, k)),
        ],
        out_specs=pl.BlockSpec((4, 16, 8, 256), lambda k: (0, 0, 0, 0)),
        scratch_shapes=[
            pltpu.VMEM((512, 256), F32),
            pltpu.VMEM((512, 256), F32),
            pltpu.VMEM((192, 256), F32),
            pltpu.VMEM((512, 128), F32),
        ],
        compiler_params=params(),
        name="products",
    )(place, *u, *v, s)


def per_device(train, test):
    t = spread(train)
    s = spread(test).reshape(4, 48, 4096)
    a2a = functools.partial(lax.all_to_all, split_axis=0, concat_axis=0, tiled=True)
    u = a2a(t[:, 0], "row")
    v_in, u = lax.optimization_barrier((t[:, 1], u))
    v = a2a(v_in, "row")
    u_other = swap(u)
    s_in, v, u_other = lax.optimization_barrier((s, v, u_other))
    s = a2a(s_in, "row")
    v_other = swap(v)

    def gather(own, other):
        near = around(jnp.concatenate([own, other]))
        far = around(near[:4])
        return own, other, near, swap(near), far, swap(far)

    x, core = lax.axis_index("x"), lax.axis_index("core")
    step = 1 - 2 * core
    x_of = jnp.stack([x, x, x - step, x - step, x + step, x + step, x + 2, x + 2]) % 4
    core_of = jnp.stack([core, 1 - core, core, 1 - core, 1 - core, core, core, 1 - core])
    place = (2 * x_of + core_of).astype(jnp.int32)
    pieces = products(place, gather(u, u_other), gather(v, v_other), s)
    parts = a2a(pieces.reshape(64, 8, 256), ("row",) + DEV)
    total = jnp.sum(parts, axis=0)
    g = total[:, :SPARE].reshape(8, 4, 2, 24)
    power = (g[:, :, 0] ** 2 + g[:, :, 1] ** 2).reshape(8, 96)
    tn = total[:, SPARE : SPARE + 1]
    diag = total[:4, SPARE + 1 :].reshape(4 * WINDOW)[:192].reshape(4, 2, 24)
    sn = (diag[:, 0] + diag[:, 1]).reshape(1, 96)
    block = float(AMPS) * power / (tn * sn)
    full = a2a(jnp.broadcast_to(block[None], (16, 8, 96)), DEV)
    return full.reshape(128, 96)


def solution(mesh):
    axes = ("row", "x", "core", "zhi", "y")
    fine = Mesh(mesh.devices.reshape(4, 4, 2, 2, 8), axes)
    placed = (
        P(("row", "x", "core"), None, DEV),
        P(("x", "core", "row"), None, DEV),
    )
    return jax.shard_map(
        per_device, mesh=fine, in_specs=placed, out_specs=P("row", ("x", "core")), check_vma=False
    )
```

time: 399 us -> 156 us (0.39)
  the two profiles are of different devices: /device:TPU:56 before, /device:TPU:8 now
where the time goes in v2:
time: 156 us; the launch traced here: 155 us
  blocking collectives  71.7 us (46%)
  starting transfers between devices  33.7 us (22%)
  waiting for transfers between devices  30.1 us (19%)
  local copies, waits for them, and re-layouts  10.7 us (7%)
  Pallas kernels  8.46 us (5%)
    all_to_all x1, blocking collectives, per_device(): parts = a2a(pieces.reshape(64, 8, 256), ('row',) + DEV)  32.8 us
    all_to_all x1, blocking collectives, per_device(): u = a2a(t[:, 0], 'row')  21.5 us
    ppermute x4, waiting for transfers between devices, around(): return lax.ppermute(block, ('x', 'core'), AROUND)  21.3 us
    all_to_all x1, blocking collectives, per_device(): full = a2a(jnp.broadcast_to(block[None], (16, 8, 96)), DEV)  17.3 us
    ppermute x6, starting transfers between devices, swap(): return lax.ppermute(block, 'core', SWAP)  14.7 us
    ppermute x4, starting transfers between devices, around(): return lax.ppermute(block, ('x', 'core'), AROUND)  11.2 us
    pallas_call x1, Pallas kernels, products(): pl.pallas_call(product_kernel, out_shape=jax.ShapeDtypeStruct((4, 16, 8,...  8.46 us
    reshape x4, local copies, waits for them, and re-layouts, spread(): return states.reshape(states.shape[0], 2, 4, 4096).transpose(2, 1, 0, 3)  7.12 us
  transfers between devices with their start and end apart: 12, of which 5 were waited for; matrix products, arithmetic and copies ran while one was open for 4% of the time, Pallas kernels for 0%

profile of v2, /device:TPU:8, one launch (start us, length us, event | category | flops | bytes accessed | tf_op | source)
XLA Modules:
  0.0 155.3 jit_solution(12715394137552119923)
XLA Ops:
  0.0 1.7 %reshape.92 = bf16[16,2,4,4096]{3,2,1,0:T(4,128)(2,1)S(1)} reshape(bf16[16,2,16384]{2,1,0:T(2,128)(2,1)} %param.2) | data formatting | bytes 2097152 | tf_op jit(solution)/shard_map/reshape | solution.py:26
  3.2 21.5 %all_to_all.25.refs_0_ = bf16[4,16,4096]{2,1,0:T(8,128)(2,1)S(1)} all-to-all(bf16[4,16,4096]{2,1,0:T(8,128)(2,1)S(1)} %get-tuple-element.15), channel_id=1, replica_groups=mesh['row'=4,'x'=4,'core'=2,'zhi'=2,'y'=8] {'row'}, dimensions={0} | all-to-all | bytes 1048576 | tf_op jit(solution)/shard_map/all_to_all | solution.py:114
  24.7 3.5 %all-to-all-start.1 = ((bf16[4,16,4096]{2,1,0:T(8,128)(2,1)}), bf16[4,16,4096]{2,1,0:T(8,128)(2,1)S(1)}, u32[]{:S(2)}, u32[]{:S(2)}) async-start(bf16[4,16,4096]{2,1,0:T(8,128)(2,1)} %get-tuple-element.11), calls=%async_computation.1 | async-start | bytes 1048576 | tf_op jit(solution)/shard_map/all_to_all | solution.py:116
  28.2 1.9 %collective-permute-start = (bf16[4,16,4096]{2,1,0:T(8,128)(2,1)S(1)}, bf16[4,16,4096]{2,1,0:T(8,128)(2,1)S(1)}, u32[]{:S(2)}, u32[]{:S(2)}) collective-permute-start(bf16[4,16,4096]{2,1,0:T(8,128)(2,1)S(1)} %all_to_all.25.refs_0_), channel_id=1, source_target_pairs={{0,16},{16,0},{1,17},{17,1},{2,18},{18,2},{3,19},{19,3},{4,20},{20... | collective-permute-start | bytes 1572872 | tf_op jit(solution)/shard_map/ppermute | solution.py:30
  30.1 2.8 %reshape.85 = bf16[24,2,4,4096]{3,2,1,0:T(4,128)(2,1)S(1)} reshape(bf16[24,2,16384]{2,1,0:T(2,128)(2,1)} %param.3) | data formatting | bytes 3145728 | tf_op jit(solution)/shard_map/reshape | solution.py:26
  32.9 2.0 %copy.10 = bf16[24,2,4,4096]{3,0,1,2:T(8,128)(2,1)} copy(bf16[24,2,4,4096]{3,2,1,0:T(4,128)(2,1)S(1)} %reshape.85) | data formatting | bytes 3145728 | tf_op jit(solution)/shard_map/reshape | solution.py:26
  35.0 6.9 %all-to-all-done.1.refs_6_ = bf16[4,16,4096]{2,1,0:T(8,128)(2,1)S(1)} async-done(((bf16[4,16,4096]{2,1,0:T(8,128)(2,1)}), bf16[4,16,4096]{2,1,0:T(8,128)(2,1)S(1)}, u32[]{:S(2)}, u32[]{:S(2)}) %all-to-all-start.1) | async-done | bytes 524320 | tf_op jit(solution)/shard_map/all_to_all | solution.py:116
  41.8 1.9 %collective-permute-start.5 = (bf16[4,16,4096]{2,1,0:T(8,128)(2,1)S(1)}, bf16[4,16,4096]{2,1,0:T(8,128)(2,1)S(1)}, u32[]{:S(2)}, u32[]{:S(2)}) collective-permute-start(bf16[4,16,4096]{2,1,0:T(8,128)(2,1)S(1)} %all-to-all-done.1.refs_6_), channel_id=1, source_target_pairs={{0,16},{16,0},{1,17},{17,1},{2,18},{18,2},{3,19},{19,3},{4,20},{20... | collective-permute-start | bytes 1572872 | tf_op jit(solution)/shard_map/ppermute | solution.py:30
  43.7 4.4 %all-to-all-start.2 = ((bf16[4,48,4096]{2,1,0:T(8,128)(2,1)}), bf16[4,48,4096]{2,1,0:T(8,128)(2,1)}, u32[]{:S(2)}, u32[]{:S(2)}) async-start(bf16[4,48,4096]{2,1,0:T(8,128)(2,1)} %bitcast.21), calls=%async_computation.2 | async-start | bytes 3145728 | tf_op jit(solution)/shard_map/all_to_all | solution.py:119
  48.2 3.4 %collective-permute-start.1 = (bf16[8,16,4096]{2,1,0:T(8,128)(2,1)S(1)}, bf16[8,16,4096]{2,1,0:T(8,128)(2,1)S(1)}, u32[]{:S(2)}, u32[]{:S(2)}) collective-permute-start(bf16[8,16,4096]{2,1,0:T(8,128)(2,1)S(1)} %pad_maximum_fusion), channel_id=1, source_target_pairs={{0,32},{16,112},{32,64},{48,16},{64,96},{80,48},{96,0},{112,80},{1... | collective-permute-start | bytes 3145736 | tf_op jit(solution)/shard_map/ppermute | solution.py:34
  51.7 3.4 %collective-permute-start.6 = (bf16[8,16,4096]{2,1,0:T(8,128)(2,1)S(1)}, bf16[8,16,4096]{2,1,0:T(8,128)(2,1)}, u32[]{:S(2)}, u32[]{:S(2)}) collective-permute-start(bf16[8,16,4096]{2,1,0:T(8,128)(2,1)S(1)} %pad_maximum_fusion.1), channel_id=1, source_target_pairs={{0,32},{16,112},{32,64},{48,16},{64,96},{80,48},{96,0},{112,80},{1... | collective-permute-start | bytes 3145736 | tf_op jit(solution)/shard_map/ppermute | solution.py:34
  55.1 11.0 %collective-permute-done.1.refs_2_ = bf16[8,16,4096]{2,1,0:T(8,128)(2,1)S(1)} collective-permute-done((bf16[8,16,4096]{2,1,0:T(8,128)(2,1)S(1)}, bf16[8,16,4096]{2,1,0:T(8,128)(2,1)S(1)}, u32[]{:S(2)}, u32[]{:S(2)}) %collective-permute-start.1) | collective-permute-done | bytes 1048608 | tf_op jit(solution)/shard_map/ppermute | solution.py:34
  66.1 2.2 %collective-permute-start.3 = (bf16[4,16,4096]{2,1,0:T(8,128)(2,1)S(1)}, bf16[4,16,4096]{2,1,0:T(8,128)(2,1)}, u32[]{:S(2)}, u32[]{:S(2)}) collective-permute-start(bf16[4,16,4096]{2,1,0:T(8,128)(2,1)S(1)} %slice.50), channel_id=1, source_target_pairs={{0,32},{16,112},{32,64},{48,16},{64,96},{80,48},{96,0},{112,80},{1... | collective-permute-start | bytes 1572872 | tf_op jit(solution)/shard_map/ppermute | solution.py:34
  68.3 3.5 %collective-permute-start.2 = (bf16[8,16,4096]{2,1,0:T(8,128)(2,1)S(1)}, bf16[8,16,4096]{2,1,0:T(8,128)(2,1)}, u32[]{:S(2)}, u32[]{:S(2)}) collective-permute-start(bf16[8,16,4096]{2,1,0:T(8,128)(2,1)S(1)} %collective-permute-done.1.refs_2_), channel_id=1, source_target_pairs={{0,16},{16,0},{1,17},{17,1},{2,18},{18,2},{3,19},{19,3},{4,20},{20... | collective-permute-start | bytes 3145736 | tf_op jit(solution)/shard_map/ppermute | solution.py:30
  71.8 5.6 %collective-permute-done.6.refs_8_ = bf16[8,16,4096]{2,1,0:T(8,128)(2,1)} collective-permute-done((bf16[8,16,4096]{2,1,0:T(8,128)(2,1)S(1)}, bf16[8,16,4096]{2,1,0:T(8,128)(2,1)}, u32[]{:S(2)}, u32[]{:S(2)}) %collective-permute-start.6) | collective-permute-done | bytes 1048608 | tf_op jit(solution)/shard_map/ppermute | solution.py:34
  78.5 2.2 %collective-permute-start.8 = (bf16[4,16,4096]{2,1,0:T(8,128)(2,1)S(1)}, bf16[4,16,4096]{2,1,0:T(8,128)(2,1)}, u32[]{:S(2)}, u32[]{:S(2)}) collective-permute-start(bf16[4,16,4096]{2,1,0:T(8,128)(2,1)S(1)} %slice.51), channel_id=1, source_target_pairs={{0,32},{16,112},{32,64},{48,16},{64,96},{80,48},{96,0},{112,80},{1... | collective-permute-start | bytes 1572872 | tf_op jit(solution)/shard_map/ppermute | solution.py:34
  80.7 3.6 %collective-permute-start.7 = (bf16[8,16,4096]{2,1,0:T(8,128)(2,1)}, bf16[8,16,4096]{2,1,0:T(8,128)(2,1)}, u32[]{:S(2)}, u32[]{:S(2)}) collective-permute-start(bf16[8,16,4096]{2,1,0:T(8,128)(2,1)} %collective-permute-done.6.refs_8_), channel_id=1, source_target_pairs={{0,16},{16,0},{1,17},{17,1},{2,18},{18,2},{3,19},{19,3},{4,20},{20... | collective-permute-start | bytes 3145736 | tf_op jit(solution)/shard_map/ppermute | solution.py:30
  84.3 1.9 %collective-permute-start.4 = (bf16[4,16,4096]{2,1,0:T(8,128)(2,1)}, bf16[4,16,4096]{2,1,0:T(8,128)(2,1)}, u32[]{:S(2)}, u32[]{:S(2)}) collective-permute-start(bf16[4,16,4096]{2,1,0:T(8,128)(2,1)} %collective-permute-done.3.refs_4_), channel_id=1, source_target_pairs={{0,16},{16,0},{1,17},{17,1},{2,18},{18,2},{3,19},{19,3},{4,20},{20... | collective-permute-start | bytes 1572872 | tf_op jit(solution)/shard_map/ppermute | solution.py:30
  86.3 4.7 %collective-permute-done.8.refs_10_ = bf16[4,16,4096]{2,1,0:T(8,128)(2,1)} collective-permute-done((bf16[4,16,4096]{2,1,0:T(8,128)(2,1)S(1)}, bf16[4,16,4096]{2,1,0:T(8,128)(2,1)}, u32[]{:S(2)}, u32[]{:S(2)}) %collective-permute-start.8) | collective-permute-done | bytes 524320 | tf_op jit(solution)/shard_map/ppermute | solution.py:34
  90.9 1.9 %collective-permute-start.9 = (bf16[4,16,4096]{2,1,0:T(8,128)(2,1)}, bf16[4,16,4096]{2,1,0:T(8,128)(2,1)}, u32[]{:S(2)}, u32[]{:S(2)}) collective-permute-start(bf16[4,16,4096]{2,1,0:T(8,128)(2,1)} %collective-permute-done.8.refs_10_), channel_id=1, source_target_pairs={{0,16},{16,0},{1,17},{17,1},{2,18},{18,2},{3,19},{19,3},{4,20},{20... | collective-permute-start | bytes 1572872 | tf_op jit(solution)/shard_map/ppermute | solution.py:30
  93.1 2.0 %collective-permute-done.9.refs_11_ = bf16[4,16,4096]{2,1,0:T(8,128)(2,1)} collective-permute-done((bf16[4,16,4096]{2,1,0:T(8,128)(2,1)}, bf16[4,16,4096]{2,1,0:T(8,128)(2,1)}, u32[]{:S(2)}, u32[]{:S(2)}) %collective-permute-start.9) | collective-permute-done | bytes 524320 | tf_op jit(solution)/shard_map/ppermute | solution.py:30
  95.1 8.5 %products.1 = f32[4,16,8,256]{3,2,1,0:T(8,128)S(1)} custom-call(s32[8]{0:T(128)S(1)} %fusion.3.place, bf16[4,16,4096]{2,1,0:T(8,128)(2,1)S(1)} %all_to_all.25.refs_0_, bf16[4,16,4096]{2,1,0:T(8,128)(2,1)S(1)} %collective-permute-done.refs_1_, bf16[8,16,4096]{2,1,0:T(8,128)(2,1)S(1)} %collective-permute-done.1.refs_2_, ...), custom_call_target="tpu_custom_call" | custom-call | tf_op jit(solution)/shard_map/products/pallas_call | solution.py:89
  103.5 32.8 %all_to_all.26 = f32[64,8,256]{2,1,0:T(8,128)S(1)} all-to-all(f32[64,8,256]{2,1,0:T(8,128)S(1)} %bitcast.20), channel_id=1, replica_groups=mesh['row'=4,'x'=4,'core'=2,'zhi'=2,'y'=8] {'row','zhi','y'}, dimensions={0} | all-to-all | bytes 1048576 | tf_op jit(solution)/shard_map/all_to_all | solution.py:133
  137.3 17.3 %all_to_all.27 = f32[16,8,96]{2,1,0:T(8,128)S(1)} all-to-all(f32[16,8,96]{2,1,0:T(8,128)S(1)} %broadcast_in_dim.2), channel_id=1, replica_groups=mesh['row'=4,'x'=4,'core'=2,'zhi'=2,'y'=8] {'zhi','y'}, dimensions={0} | all-to-all | bytes 98304 | tf_op jit(solution)/shard_map/all_to_all | solution.py:141
  (29 shorter events, 4.6 us)
Async XLA Ops:
  24.7 17.1 %all-to-all-start.1 = ((bf16[4,16,4096]{2,1,0:T(8,128)(2,1)}), bf16[4,16,4096]{2,1,0:T(8,128)(2,1)S(1)}, u32[]{:S(2)}, u32[]{:S(2)}) async-start(bf16[4,16,4096]{2,1,0:T(8,128)(2,1)} %get-tuple-element.11), calls=%async_computation.1 | async-start | bytes 1048576 | tf_op jit(solution)/shard_map/all_to_all | solution.py:116
  28.2 6.7 %collective-permute-start = (bf16[4,16,4096]{2,1,0:T(8,128)(2,1)S(1)}, bf16[4,16,4096]{2,1,0:T(8,128)(2,1)S(1)}, u32[]{:S(2)}, u32[]{:S(2)}) collective-permute-start(bf16[4,16,4096]{2,1,0:T(8,128)(2,1)S(1)} %all_to_all.25.refs_0_), channel_id=1, source_target_pairs={{0,16},{16,0},{1,17},{17,1},{2,18},{18,2},{3,19},{19,3},{4,20},{20... | collective-permute-start | bytes 1572872 | tf_op jit(solution)/shard_map/ppermute | solution.py:30
  41.8 9.8 %collective-permute-start.5 = (bf16[4,16,4096]{2,1,0:T(8,128)(2,1)S(1)}, bf16[4,16,4096]{2,1,0:T(8,128)(2,1)S(1)}, u32[]{:S(2)}, u32[]{:S(2)}) collective-permute-start(bf16[4,16,4096]{2,1,0:T(8,128)(2,1)S(1)} %all-to-all-done.1.refs_6_), channel_id=1, source_target_pairs={{0,16},{16,0},{1,17},{17,1},{2,18},{18,2},{3,19},{19,3},{4,20},{20... | collective-permute-start | bytes 1572872 | tf_op jit(solution)/shard_map/ppermute | solution.py:30
  43.7 49.3 %all-to-all-start.2 = ((bf16[4,48,4096]{2,1,0:T(8,128)(2,1)}), bf16[4,48,4096]{2,1,0:T(8,128)(2,1)}, u32[]{:S(2)}, u32[]{:S(2)}) async-start(bf16[4,48,4096]{2,1,0:T(8,128)(2,1)} %bitcast.21), calls=%async_computation.2 | async-start | bytes 3145728 | tf_op jit(solution)/shard_map/all_to_all | solution.py:119
  48.2 17.9 %collective-permute-start.1 = (bf16[8,16,4096]{2,1,0:T(8,128)(2,1)S(1)}, bf16[8,16,4096]{2,1,0:T(8,128)(2,1)S(1)}, u32[]{:S(2)}, u32[]{:S(2)}) collective-permute-start(bf16[8,16,4096]{2,1,0:T(8,128)(2,1)S(1)} %pad_maximum_fusion), channel_id=1, source_target_pairs={{0,32},{16,112},{32,64},{48,16},{64,96},{80,48},{96,0},{112,80},{1... | collective-permute-start | bytes 3145736 | tf_op jit(solution)/shard_map/ppermute | solution.py:34
  51.7 25.7 %collective-permute-start.6 = (bf16[8,16,4096]{2,1,0:T(8,128)(2,1)S(1)}, bf16[8,16,4096]{2,1,0:T(8,128)(2,1)}, u32[]{:S(2)}, u32[]{:S(2)}) collective-permute-start(bf16[8,16,4096]{2,1,0:T(8,128)(2,1)S(1)} %pad_maximum_fusion.1), channel_id=1, source_target_pairs={{0,32},{16,112},{32,64},{48,16},{64,96},{80,48},{96,0},{112,80},{1... | collective-permute-start | bytes 3145736 | tf_op jit(solution)/shard_map/ppermute | solution.py:34
  66.1 18.2 %collective-permute-start.3 = (bf16[4,16,4096]{2,1,0:T(8,128)(2,1)S(1)}, bf16[4,16,4096]{2,1,0:T(8,128)(2,1)}, u32[]{:S(2)}, u32[]{:S(2)}) collective-permute-start(bf16[4,16,4096]{2,1,0:T(8,128)(2,1)S(1)} %slice.50), channel_id=1, source_target_pairs={{0,32},{16,112},{32,64},{48,16},{64,96},{80,48},{96,0},{112,80},{1... | collective-permute-start | bytes 1572872 | tf_op jit(solution)/shard_map/ppermute | solution.py:34
  68.3 24.7 %collective-permute-start.2 = (bf16[8,16,4096]{2,1,0:T(8,128)(2,1)S(1)}, bf16[8,16,4096]{2,1,0:T(8,128)(2,1)}, u32[]{:S(2)}, u32[]{:S(2)}) collective-permute-start(bf16[8,16,4096]{2,1,0:T(8,128)(2,1)S(1)} %collective-permute-done.1.refs_2_), channel_id=1, source_target_pairs={{0,16},{16,0},{1,17},{17,1},{2,18},{18,2},{3,19},{19,3},{4,20},{20... | collective-permute-start | bytes 3145736 | tf_op jit(solution)/shard_map/ppermute | solution.py:30
  78.5 12.4 %collective-permute-start.8 = (bf16[4,16,4096]{2,1,0:T(8,128)(2,1)S(1)}, bf16[4,16,4096]{2,1,0:T(8,128)(2,1)}, u32[]{:S(2)}, u32[]{:S(2)}) collective-permute-start(bf16[4,16,4096]{2,1,0:T(8,128)(2,1)S(1)} %slice.51), channel_id=1, source_target_pairs={{0,32},{16,112},{32,64},{48,16},{64,96},{80,48},{96,0},{112,80},{1... | collective-permute-start | bytes 1572872 | tf_op jit(solution)/shard_map/ppermute | solution.py:34
  80.7 14.3 %collective-permute-start.7 = (bf16[8,16,4096]{2,1,0:T(8,128)(2,1)}, bf16[8,16,4096]{2,1,0:T(8,128)(2,1)}, u32[]{:S(2)}, u32[]{:S(2)}) collective-permute-start(bf16[8,16,4096]{2,1,0:T(8,128)(2,1)} %collective-permute-done.6.refs_8_), channel_id=1, source_target_pairs={{0,16},{16,0},{1,17},{17,1},{2,18},{18,2},{3,19},{19,3},{4,20},{20... | collective-permute-start | bytes 3145736 | tf_op jit(solution)/shard_map/ppermute | solution.py:30
  84.3 8.7 %collective-permute-start.4 = (bf16[4,16,4096]{2,1,0:T(8,128)(2,1)}, bf16[4,16,4096]{2,1,0:T(8,128)(2,1)}, u32[]{:S(2)}, u32[]{:S(2)}) collective-permute-start(bf16[4,16,4096]{2,1,0:T(8,128)(2,1)} %collective-permute-done.3.refs_4_), channel_id=1, source_target_pairs={{0,16},{16,0},{1,17},{17,1},{2,18},{18,2},{3,19},{19,3},{4,20},{20... | collective-permute-start | bytes 1572872 | tf_op jit(solution)/shard_map/ppermute | solution.py:30
  90.9 4.1 %collective-permute-start.9 = (bf16[4,16,4096]{2,1,0:T(8,128)(2,1)}, bf16[4,16,4096]{2,1,0:T(8,128)(2,1)}, u32[]{:S(2)}, u32[]{:S(2)}) collective-permute-start(bf16[4,16,4096]{2,1,0:T(8,128)(2,1)} %collective-permute-done.8.refs_10_), channel_id=1, source_target_pairs={{0,16},{16,0},{1,17},{17,1},{2,18},{18,2},{3,19},{19,3},{4,20},{20... | collective-permute-start | bytes 1572872 | tf_op jit(solution)/shard_map/ppermute | solution.py:30

commit v3 on v0

v3 whole, which is shorter than its diff:
```python
import functools

import jax
import jax.numpy as jnp
from jax import lax
from jax.experimental import pallas as pl
from jax.experimental.pallas import tpu as pltpu
from jax.sharding import Mesh, PartitionSpec as P

AMPS = 262144
F32 = jnp.float32
DEV = ("zhi", "y")
SPARE = 192
WINDOW = 63

GROUP = 8
DEPTH = 2048
SWAP = [(0, 1), (1, 0)]
AHEAD, BACK = ([(2 * x + c, 2 * ((x + way[c]) % 4) + c) for x in range(4) for c in (0, 1)] for way in ((1, -1), (-1, 1)))


def params(mib):
    return pltpu.CompilerParams(vmem_limit_bytes=mib * 1024 * 1024)


def spread_kernel(states, out):
    for j in range(out.shape[0]):
        out[j] = states[:, :, DEPTH * j : DEPTH * (j + 1)].reshape(out.shape[1:])


def spread(states, mib):
    count = states.shape[0]
    return pl.pallas_call(
        spread_kernel,
        out_shape=jax.ShapeDtypeStruct((8, 2 * count, DEPTH), states.dtype),
        grid=(2,),
        in_specs=[pl.BlockSpec((count, 2, 4 * DEPTH), lambda g: (0, 0, g))],
        out_specs=pl.BlockSpec((4, 2 * count, DEPTH), lambda g: (g, 0, 0)),
        compiler_params=params(mib),
        name="spread",
    )(states)


def product_kernel(sizes, place, *refs):
    m = len(sizes)
    s_all, (keep, send, gg, tt) = refs[m], refs[-4:]
    core = place[2 * sum(sizes)]
    nt = (((1,), (1,)), ((), ()))
    starts = [sum(sizes[:i]) for i in range(m + 1)]
    columns, spare = [], []
    sub = lax.broadcasted_iota(jnp.int32, (8, 256), 0)
    lane8 = lax.broadcasted_iota(jnp.int32, (8, 256), 1)
    r = lax.broadcasted_iota(jnp.int32, (192, 192), 0)
    on = r == lax.broadcasted_iota(jnp.int32, (192, 192), 1)
    for of in (core, 1 - core):
        s = jnp.concatenate([s_all[pl.ds(2 * z + of, 1)] for z in range(4)], axis=0).reshape(192, DEPTH)
        columns.append(s)
        ss = lax.dot_general(s, s, nt, preferred_element_type=F32)
        diag = jnp.sum(jnp.where(on, ss, 0.0), axis=0, keepdims=True)
        diag = jnp.broadcast_to(jnp.concatenate([diag, jnp.zeros((1, 64), F32)], axis=1), (8, 256))
        rows = jnp.zeros((8, 256), F32)
        for w in range(4):
            moved = pltpu.roll(diag, (SPARE + 1 - WINDOW * w) % 256, 1)
            rows = rows + jnp.where((sub == w) & (lane8 > SPARE), moved, 0.0)
        spare.append(rows)

    done = 0
    while done < m:
        last = done + 1
        while last < m and starts[last] - starts[done] < GROUP:
            last += 1
        a, n = starts[done], starts[last] - starts[done]
        t = jnp.concatenate([ref[...] for ref in refs[done:last]], axis=0).reshape(32 * n, DEPTH)
        done = last
        total = jnp.zeros((32 * n, 128), F32)
        for j in range(DEPTH // 128):
            x = t[:, 128 * j : 128 * j + 128].astype(F32)
            total = total + x * x
        at = pl.ds(32 * a, 32 * n)
        tt[at, :] = total
        even, odd = pl.ds(32 * a, 16 * n, stride=2), pl.ds(32 * a + 1, 16 * n, stride=2)
        tn = jnp.sum(tt[even, :] + tt[odd, :], axis=1, keepdims=True)
        lane = lax.broadcasted_iota(jnp.int32, (16 * n, 256), 1)
        first = lane % 2 == 0
        for c, out in enumerate((keep, send)):
            g = lax.dot_general(t, columns[c], nt, preferred_element_type=F32)
            gg[2 * c, at, :] = g[:, :128]
            gg[2 * c + 1, at, :] = jnp.concatenate([g[:, 128:], jnp.zeros((32 * n, 64), F32)], axis=1)
            gu, gv = (jnp.concatenate([gg[2 * c, rows, :], gg[2 * c + 1, rows, :]], axis=1) for rows in (even, odd))
            both = gu + jnp.where(first, pltpu.roll(gv, 255, 1), -pltpu.roll(gv, 1, 1))
            both = jnp.where(lane < SPARE, both, jnp.where(lane == SPARE, tn, 0.0))
            both = (both.reshape(2 * n, 8, 256) + spare[c][None]).reshape(n, 2, 8, 256)
            for j in range(n):
                out[pl.ds(place[a + j], 1), pl.ds(place[sum(sizes) + a + j], 2)] = both[j : j + 1]


def products(at, core, blocks, s):
    n = len(at)
    place = jnp.stack([r for _, r, _ in at] + [4 * x + 2 * c for x, _, c in at] + [core]).astype(jnp.int32)
    out = pl.BlockSpec((4, 16, 8, 256), lambda k, place: (0, 0, 0, 0))
    return pl.pallas_call(
        functools.partial(product_kernel, [b.shape[0] for b in blocks]),
        out_shape=[jax.ShapeDtypeStruct((4, 16, 8, 256), F32)] * 2,
        grid_spec=pltpu.PrefetchScalarGridSpec(
            num_scalar_prefetch=1,
            grid=(1,),
            in_specs=[pl.BlockSpec(memory_space=pltpu.VMEM)] * (len(blocks) + 1),
            out_specs=[out] * 2,
            scratch_shapes=[
                pltpu.VMEM((4, 32 * n, 128), F32),
                pltpu.VMEM((32 * n, 128), F32),
            ],
        ),
        cost_estimate=pl.CostEstimate(flops=2 * 32 * n * 384 * DEPTH, bytes_accessed=64 * n * DEPTH, transcendentals=0),
        compiler_params=params(24),
        name="products",
    )(place, *blocks, s)


def per_device(train, test):
    a2a = functools.partial(lax.all_to_all, split_axis=0, concat_axis=0, tiled=True)
    x, core, row = lax.axis_index("x"), lax.axis_index("core"), lax.axis_index("row")
    held = spread(train, 60)
    t = a2a(held, ("row", "core"))

    def around(own):
        first = lax.ppermute(own, ("x", "core"), AHEAD)
        return first, lax.ppermute(own, ("x", "core"), BACK), lax.ppermute(first, ("x", "core"), AHEAD)

    mine, theirs = (lax.dynamic_slice_in_dim(held, 2 * row + c, 1, 0) for c in (core, 1 - core))
    stay = around(jnp.concatenate([mine, lax.ppermute(theirs, "core", SWAP)]))
    s, t, stay = lax.optimization_barrier((spread(test, 16), t, jnp.concatenate(stay)))
    s = a2a(s, ("row", "core"))
    others = [(row + k) % 4 for k in (1, 2, 3)]
    come = around(jnp.concatenate([lax.dynamic_slice_in_dim(t, 2 * r, 2, 0) for r in others]))
    stay_at = [(row, core), (row, 1 - core)]
    come_at = [(r, c) for r in others for c in (0, 1)]
    at = [(x, r, c) for r in range(4) for c in (0, 1)]
    for there in (stay_at, come_at):
        at += [((x + dx + 4) % 4, r, c) for dx in (2 * core - 1, 1 - 2 * core, 2) for r, c in there]
    keep, send = products(at, core, (t, stay, *come), s)
    pieces = keep + lax.ppermute(send, "core", SWAP)
    parts = a2a(pieces.reshape(64, 8, 256), ("row",) + DEV)
    total = jnp.sum(parts, axis=0)
    power = jnp.sum((total[:, :SPARE] ** 2).reshape(8, 96, 2), axis=2)
    tn = total[:, SPARE : SPARE + 1]
    diag = total[:4, SPARE + 1 :].reshape(4 * WINDOW)[:192]
    sn = jnp.sum(diag.reshape(1, 96, 2), axis=2)
    block = float(AMPS) * power / (tn * sn)
    full = a2a(jnp.broadcast_to(block[None], (16, 8, 96)), DEV)
    return full.reshape(128, 96)


def solution(mesh):
    axes = ("row", "x", "core", "zhi", "y")
    fine = Mesh(mesh.devices.reshape(4, 4, 2, 2, 8), axes)
    placed = (
        P(("row", "x", "core"), None, DEV),
        P(("x", "core", "row"), None, DEV),
    )
    return jax.shard_map(
        per_device, mesh=fine, in_specs=placed, out_specs=P("row", ("x", "core")), check_vma=False
    )
```

time: 399 us -> 140 us (0.35)
  the two profiles are of different devices: /device:TPU:56 before, /device:TPU:2 now
where the time goes in v3:
time: 140 us; the launch traced here: 139 us
  blocking collectives  50.2 us (36%)
  waiting for transfers between devices  39.6 us (28%)
  starting transfers between devices  35.7 us (26%)
  Pallas kernels  9.32 us (7%)
  local copies, waits for them, and re-layouts  2.47 us (2%)
  other arithmetic  1.54 us (1%)
    all_to_all x1, blocking collectives, per_device(): parts = a2a(pieces.reshape(64, 8, 256), ('row',) + DEV)  32.1 us
    all_to_all x1, blocking collectives, per_device(): full = a2a(jnp.broadcast_to(block[None], (16, 8, 96)), DEV)  18.1 us
    ppermute x2, waiting for transfers between devices, around(): lax.ppermute(first, ('x', 'core'), AHEAD)  16.1 us
    ppermute x2, waiting for transfers between devices, around(): first = lax.ppermute(own, ('x', 'core'), AHEAD)  16.1 us
    ppermute x2, starting transfers between devices, around(): lax.ppermute(first, ('x', 'core'), AHEAD)  8.47 us
    all_to_all x1, starting transfers between devices, per_device(): t = a2a(held, ('row', 'core'))  7.4 us
    ppermute x2, starting transfers between devices, around(): first = lax.ppermute(own, ('x', 'core'), AHEAD)  6.79 us
    pallas_call x1, Pallas kernels, products(): pl.pallas_call(functools.partial(product_kernel, [b.shape[0] for b in blo...  5.87 us
  transfers between devices with their start and end apart: 10, of which 8 were waited for; matrix products, arithmetic and copies ran while one was open for 2% of the time, Pallas kernels for 1%

profile of v3, /device:TPU:2, one launch (start us, length us, event | category | flops | bytes accessed | tf_op | source)
XLA Modules:
  0.0 139.0 jit_solution(4159460003644658339)
XLA Ops:
  0.0 2.1 %spread.3 = bf16[8,32,2048]{2,1,0:T(8,128)(2,1)} custom-call(bf16[16,2,16384]{2,1,0:T(2,128)(2,1)} %states.3), custom_call_target="tpu_custom_call" | custom-call | tf_op jit(solution)/shard_map/spread/pallas_call | solution.py:33
  2.1 7.4 %all-to-all-start = ((bf16[8,32,2048]{2,1,0:T(8,128)(2,1)}), bf16[8,32,2048]{2,1,0:T(8,128)(2,1)S(1)}, u32[]{:S(2)}, u32[]{:S(2)}) async-start(bf16[8,32,2048]{2,1,0:T(8,128)(2,1)} %spread.3), calls=%async_computation | async-start | bytes 2097152 | tf_op jit(solution)/shard_map/all_to_all | solution.py:124
  9.5 1.0 constant_dynamic-slice_fusion.4
  10.4 2.4 %collective-permute-start = (bf16[1,32,2048]{2,1,0:T(8,128)(2,1)S(1)}, bf16[1,32,2048]{2,1,0:T(8,128)(2,1)S(1)}, u32[]{:S(2)}, u32[]{:S(2)}) collective-permute-start(bf16[1,32,2048]{2,1,0:T(8,128)(2,1)S(1)} %get-tuple-element.19), channel_id=1, source_target_pairs={{0,16},{16,0},{1,17},{17,1},{2,18},{18,2},{3,19},{19,3},{4,20},{20... | collective-permute-start | bytes 393224 | tf_op jit(solution)/shard_map/ppermute | solution.py:131
  12.9 1.0 collective-permute-done
  13.9 3.4 %collective-permute-start.1 = (bf16[2,32,2048]{2,1,0:T(8,128)(2,1)S(1)}, bf16[2,32,2048]{2,1,0:T(8,128)(2,1)S(1)}, u32[]{:S(2)}, u32[]{:S(2)}) collective-permute-start(bf16[2,32,2048]{2,1,0:T(8,128)(2,1)S(1)} %pad_maximum_fusion.2), channel_id=1, source_target_pairs={{0,32},{16,112},{32,64},{48,16},{64,96},{80,48},{96,0},{112,80},{1... | collective-permute-start | bytes 786440 | tf_op jit(solution)/shard_map/ppermute | solution.py:127
  17.3 2.5 %collective-permute-start.2 = (bf16[2,32,2048]{2,1,0:T(8,128)(2,1)S(1)}, bf16[2,32,2048]{2,1,0:T(8,128)(2,1)S(1)}, u32[]{:S(2)}, u32[]{:S(2)}) collective-permute-start(bf16[2,32,2048]{2,1,0:T(8,128)(2,1)S(1)} %pad_maximum_fusion.2), channel_id=1, source_target_pairs={{0,96},{16,48},{32,0},{48,80},{64,32},{80,112},{96,64},{112,16},{1... | collective-permute-start | bytes 786440 | tf_op jit(solution)/shard_map/ppermute | solution.py:128
  19.8 2.4 %collective-permute-done.1 = bf16[2,32,2048]{2,1,0:T(8,128)(2,1)S(1)} collective-permute-done((bf16[2,32,2048]{2,1,0:T(8,128)(2,1)S(1)}, bf16[2,32,2048]{2,1,0:T(8,128)(2,1)S(1)}, u32[]{:S(2)}, u32[]{:S(2)}) %collective-permute-start.1) | collective-permute-done | bytes 262176 | tf_op jit(solution)/shard_map/ppermute | solution.py:127
  22.2 4.1 %collective-permute-start.3 = (bf16[2,32,2048]{2,1,0:T(8,128)(2,1)S(1)}, bf16[2,32,2048]{2,1,0:T(8,128)(2,1)S(1)}, u32[]{:S(2)}, u32[]{:S(2)}) collective-permute-start(bf16[2,32,2048]{2,1,0:T(8,128)(2,1)S(1)} %collective-permute-done.1), channel_id=1, source_target_pairs={{0,32},{16,112},{32,64},{48,16},{64,96},{80,48},{96,0},{112,80},{1... | collective-permute-start | bytes 786440 | tf_op jit(solution)/shard_map/ppermute | solution.py:128
  26.3 1.4 %spread.2 = bf16[8,48,2048]{2,1,0:T(8,128)(2,1)} custom-call(bf16[24,2,16384]{2,1,0:T(2,128)(2,1)S(1)} %copy-done), custom_call_target="tpu_custom_call" | custom-call | tf_op jit(solution)/shard_map/spread/pallas_call | solution.py:33
  27.7 4.5 %collective-permute-done.3 = bf16[2,32,2048]{2,1,0:T(8,128)(2,1)S(1)} collective-permute-done((bf16[2,32,2048]{2,1,0:T(8,128)(2,1)S(1)}, bf16[2,32,2048]{2,1,0:T(8,128)(2,1)S(1)}, u32[]{:S(2)}, u32[]{:S(2)}) %collective-permute-start.3) | collective-permute-done | bytes 262176 | tf_op jit(solution)/shard_map/ppermute | solution.py:128
  32.3 3.8 %all-to-all-done.refs_0_ = bf16[8,32,2048]{2,1,0:T(8,128)(2,1)S(1)} async-done(((bf16[8,32,2048]{2,1,0:T(8,128)(2,1)}), bf16[8,32,2048]{2,1,0:T(8,128)(2,1)S(1)}, u32[]{:S(2)}, u32[]{:S(2)}) %all-to-all-start) | async-done | bytes 1048608 | tf_op jit(solution)/shard_map/all_to_all | solution.py:124
  36.1 3.6 %all-to-all-start.1 = ((bf16[8,48,2048]{2,1,0:T(8,128)(2,1)}), bf16[8,48,2048]{2,1,0:T(8,128)(2,1)S(1)}, u32[]{:S(2)}, u32[]{:S(2)}) async-start(bf16[8,48,2048]{2,1,0:T(8,128)(2,1)} %spread.2), calls=%async_computation.1 | async-start | bytes 3145728 | tf_op jit(solution)/shard_map/all_to_all | solution.py:133
  39.8 1.0 pad_maximum_fusion.1
  40.7 3.4 %collective-permute-start.4 = (bf16[6,32,2048]{2,1,0:T(8,128)(2,1)}, bf16[6,32,2048]{2,1,0:T(8,128)(2,1)}, u32[]{:S(2)}, u32[]{:S(2)}) collective-permute-start(bf16[6,32,2048]{2,1,0:T(8,128)(2,1)} %pad_maximum_fusion.1), channel_id=1, source_target_pairs={{0,32},{16,112},{32,64},{48,16},{64,96},{80,48},{96,0},{112,80},{1... | collective-permute-start | bytes 2359304 | tf_op jit(solution)/shard_map/ppermute | solution.py:127
  44.1 2.6 %collective-permute-start.5 = (bf16[6,32,2048]{2,1,0:T(8,128)(2,1)}, bf16[6,32,2048]{2,1,0:T(8,128)(2,1)}, u32[]{:S(2)}, u32[]{:S(2)}) collective-permute-start(bf16[6,32,2048]{2,1,0:T(8,128)(2,1)} %pad_maximum_fusion.1), channel_id=1, source_target_pairs={{0,96},{16,48},{32,0},{48,80},{64,32},{80,112},{96,64},{112,16},{1... | collective-permute-start | bytes 2359304 | tf_op jit(solution)/shard_map/ppermute | solution.py:128
  46.7 13.7 %collective-permute-done.4.refs_2_ = bf16[6,32,2048]{2,1,0:T(8,128)(2,1)} collective-permute-done((bf16[6,32,2048]{2,1,0:T(8,128)(2,1)}, bf16[6,32,2048]{2,1,0:T(8,128)(2,1)}, u32[]{:S(2)}, u32[]{:S(2)}) %collective-permute-start.4) | collective-permute-done | bytes 786464 | tf_op jit(solution)/shard_map/ppermute | solution.py:127
  60.4 4.4 %collective-permute-start.6 = (bf16[6,32,2048]{2,1,0:T(8,128)(2,1)}, bf16[6,32,2048]{2,1,0:T(8,128)(2,1)}, u32[]{:S(2)}, u32[]{:S(2)}) collective-permute-start(bf16[6,32,2048]{2,1,0:T(8,128)(2,1)} %collective-permute-done.4.refs_2_), channel_id=1, source_target_pairs={{0,32},{16,112},{32,64},{48,16},{64,96},{80,48},{96,0},{112,80},{1... | collective-permute-start | bytes 2359304 | tf_op jit(solution)/shard_map/ppermute | solution.py:128
  65.0 11.6 %collective-permute-done.6.refs_4_ = bf16[6,32,2048]{2,1,0:T(8,128)(2,1)} collective-permute-done((bf16[6,32,2048]{2,1,0:T(8,128)(2,1)}, bf16[6,32,2048]{2,1,0:T(8,128)(2,1)}, u32[]{:S(2)}, u32[]{:S(2)}) %collective-permute-start.6) | collective-permute-done | bytes 786464 | tf_op jit(solution)/shard_map/ppermute | solution.py:128
  77.4 5.9 %products.1 = (f32[4,16,8,256]{3,2,1,0:T(8,128)S(1)}, f32[4,16,8,256]{3,2,1,0:T(8,128)S(1)}) custom-call(s32[65]{0:T(128)S(1)} %stack.117.place, bf16[8,32,2048]{2,1,0:T(8,128)(2,1)S(1)} %all-to-all-done.refs_0_, bf16[6,32,2048]{2,1,0:T(8,128)(2,1)S(1)} %pad_maximum_fusion.refs_1_, bf16[6,32,2048]{2,1,0:T(8,128)(2,1)} %collective-permute-done.4.refs_2_, ...), custom_call_target="tpu_custom_call" | custom-call | flops 1610612736 | bytes 4194304 | tf_op jit(solution)/shard_map/products/pallas_call | solution.py:101
  83.3 1.9 %collective-permute-start.7 = (f32[4,16,8,256]{3,2,1,0:T(8,128)S(1)}, f32[4,16,8,256]{3,2,1,0:T(8,128)S(1)}, u32[]{:S(2)}, u32[]{:S(2)}) collective-permute-start(f32[4,16,8,256]{3,2,1,0:T(8,128)S(1)} %get-tuple-element.14), channel_id=1, source_target_pairs={{0,16},{16,0},{1,17},{17,1},{2,18},{18,2},{3,19},{19,3},{4,20},{20... | collective-permute-start | bytes 1572872 | tf_op jit(solution)/shard_map/ppermute | solution.py:142
  85.2 1.9 %collective-permute-done.7 = f32[4,16,8,256]{3,2,1,0:T(8,128)S(1)} collective-permute-done((f32[4,16,8,256]{3,2,1,0:T(8,128)S(1)}, f32[4,16,8,256]{3,2,1,0:T(8,128)S(1)}, u32[]{:S(2)}, u32[]{:S(2)}) %collective-permute-start.7) | collective-permute-done | bytes 524320 | tf_op jit(solution)/shard_map/ppermute | solution.py:142
  87.1 32.1 %all_to_all.20 = f32[64,8,256]{2,1,0:T(8,128)S(1)} all-to-all(f32[64,8,256]{2,1,0:T(8,128)S(1)} %bitcast.22), channel_id=1, replica_groups=mesh['row'=4,'x'=4,'core'=2,'zhi'=2,'y'=8] {'row','zhi','y'}, dimensions={0} | all-to-all | bytes 1048576 | tf_op jit(solution)/shard_map/all_to_all | solution.py:143
  120.2 18.1 %all_to_all.21 = f32[16,8,96]{2,1,0:T(8,128)S(1)} all-to-all(f32[16,8,96]{2,1,0:T(8,128)S(1)} %broadcast_in_dim.2), channel_id=1, replica_groups=mesh['row'=4,'x'=4,'core'=2,'zhi'=2,'y'=8] {'zhi','y'}, dimensions={0} | all-to-all | bytes 98304 | tf_op jit(solution)/shard_map/all_to_all | solution.py:150
  (26 shorter events, 2.8 us)
Async XLA Ops:
  2.1 24.3 %copy-start = (bf16[24,2,16384]{2,1,0:T(2,128)(2,1)S(1)}, bf16[24,2,16384]{2,1,0:T(2,128)(2,1)}, u32[]{:S(2)}) copy-start(bf16[24,2,16384]{2,1,0:T(2,128)(2,1)} %states.2) | copy-start | bytes 4718596
  2.1 34.0 %all-to-all-start = ((bf16[8,32,2048]{2,1,0:T(8,128)(2,1)}), bf16[8,32,2048]{2,1,0:T(8,128)(2,1)S(1)}, u32[]{:S(2)}, u32[]{:S(2)}) async-start(bf16[8,32,2048]{2,1,0:T(8,128)(2,1)} %spread.3), calls=%async_computation | async-start | bytes 2097152 | tf_op jit(solution)/shard_map/all_to_all | solution.py:124
  10.4 3.4 %collective-permute-start = (bf16[1,32,2048]{2,1,0:T(8,128)(2,1)S(1)}, bf16[1,32,2048]{2,1,0:T(8,128)(2,1)S(1)}, u32[]{:S(2)}, u32[]{:S(2)}) collective-permute-start(bf16[1,32,2048]{2,1,0:T(8,128)(2,1)S(1)} %get-tuple-element.19), channel_id=1, source_target_pairs={{0,16},{16,0},{1,17},{17,1},{2,18},{18,2},{3,19},{19,3},{4,20},{20... | collective-permute-start | bytes 393224 | tf_op jit(solution)/shard_map/ppermute | solution.py:131
  13.9 8.4 %collective-permute-start.1 = (bf16[2,32,2048]{2,1,0:T(8,128)(2,1)S(1)}, bf16[2,32,2048]{2,1,0:T(8,128)(2,1)S(1)}, u32[]{:S(2)}, u32[]{:S(2)}) collective-permute-start(bf16[2,32,2048]{2,1,0:T(8,128)(2,1)S(1)} %pad_maximum_fusion.2), channel_id=1, source_target_pairs={{0,32},{16,112},{32,64},{48,16},{64,96},{80,48},{96,0},{112,80},{1... | collective-permute-start | bytes 786440 | tf_op jit(solution)/shard_map/ppermute | solution.py:127
  17.3 10.5 %collective-permute-start.2 = (bf16[2,32,2048]{2,1,0:T(8,128)(2,1)S(1)}, bf16[2,32,2048]{2,1,0:T(8,128)(2,1)S(1)}, u32[]{:S(2)}, u32[]{:S(2)}) collective-permute-start(bf16[2,32,2048]{2,1,0:T(8,128)(2,1)S(1)} %pad_maximum_fusion.2), channel_id=1, source_target_pairs={{0,96},{16,48},{32,0},{48,80},{64,32},{80,112},{96,64},{112,16},{1... | collective-permute-start | bytes 786440 | tf_op jit(solution)/shard_map/ppermute | solution.py:128
  22.2 10.0 %collective-permute-start.3 = (bf16[2,32,2048]{2,1,0:T(8,128)(2,1)S(1)}, bf16[2,32,2048]{2,1,0:T(8,128)(2,1)S(1)}, u32[]{:S(2)}, u32[]{:S(2)}) collective-permute-start(bf16[2,32,2048]{2,1,0:T(8,128)(2,1)S(1)} %collective-permute-done.1), channel_id=1, source_target_pairs={{0,32},{16,112},{32,64},{48,16},{64,96},{80,48},{96,0},{112,80},{1... | collective-permute-start | bytes 786440 | tf_op jit(solution)/shard_map/ppermute | solution.py:128
  36.1 41.3 %all-to-all-start.1 = ((bf16[8,48,2048]{2,1,0:T(8,128)(2,1)}), bf16[8,48,2048]{2,1,0:T(8,128)(2,1)S(1)}, u32[]{:S(2)}, u32[]{:S(2)}) async-start(bf16[8,48,2048]{2,1,0:T(8,128)(2,1)} %spread.2), calls=%async_computation.1 | async-start | bytes 3145728 | tf_op jit(solution)/shard_map/all_to_all | solution.py:133
  40.7 19.6 %collective-permute-start.4 = (bf16[6,32,2048]{2,1,0:T(8,128)(2,1)}, bf16[6,32,2048]{2,1,0:T(8,128)(2,1)}, u32[]{:S(2)}, u32[]{:S(2)}) collective-permute-start(bf16[6,32,2048]{2,1,0:T(8,128)(2,1)} %pad_maximum_fusion.1), channel_id=1, source_target_pairs={{0,32},{16,112},{32,64},{48,16},{64,96},{80,48},{96,0},{112,80},{1... | collective-permute-start | bytes 2359304 | tf_op jit(solution)/shard_map/ppermute | solution.py:127
  44.1 20.8 %collective-permute-start.5 = (bf16[6,32,2048]{2,1,0:T(8,128)(2,1)}, bf16[6,32,2048]{2,1,0:T(8,128)(2,1)}, u32[]{:S(2)}, u32[]{:S(2)}) collective-permute-start(bf16[6,32,2048]{2,1,0:T(8,128)(2,1)} %pad_maximum_fusion.1), channel_id=1, source_target_pairs={{0,96},{16,48},{32,0},{48,80},{64,32},{80,112},{96,64},{112,16},{1... | collective-permute-start | bytes 2359304 | tf_op jit(solution)/shard_map/ppermute | solution.py:128
  60.4 16.2 %collective-permute-start.6 = (bf16[6,32,2048]{2,1,0:T(8,128)(2,1)}, bf16[6,32,2048]{2,1,0:T(8,128)(2,1)}, u32[]{:S(2)}, u32[]{:S(2)}) collective-permute-start(bf16[6,32,2048]{2,1,0:T(8,128)(2,1)} %collective-permute-done.4.refs_2_), channel_id=1, source_target_pairs={{0,32},{16,112},{32,64},{48,16},{64,96},{80,48},{96,0},{112,80},{1... | collective-permute-start | bytes 2359304 | tf_op jit(solution)/shard_map/ppermute | solution.py:128
  83.3 3.8 %collective-permute-start.7 = (f32[4,16,8,256]{3,2,1,0:T(8,128)S(1)}, f32[4,16,8,256]{3,2,1,0:T(8,128)S(1)}, u32[]{:S(2)}, u32[]{:S(2)}) collective-permute-start(f32[4,16,8,256]{3,2,1,0:T(8,128)S(1)} %get-tuple-element.14), channel_id=1, source_target_pairs={{0,16},{16,0},{1,17},{17,1},{2,18},{18,2},{3,19},{19,3},{4,20},{20... | collective-permute-start | bytes 1572872 | tf_op jit(solution)/shard_map/ppermute | solution.py:142

commit v4 on v3

v4 whole, which is shorter than its diff:
```python
import functools

import jax
import jax.numpy as jnp
from jax import lax
from jax.experimental import pallas as pl
from jax.experimental.pallas import tpu as pltpu
from jax.sharding import Mesh, PartitionSpec as P

AMPS = 262144
F32 = jnp.float32
DEV = ("zhi", "y")
SPARE = 192
WINDOW = 63

GROUP = 7
DEPTH = 4096
SWAP = [(0, 1), (1, 0)]
AHEAD, BACK = ([(2 * x + c, 2 * ((x + way[c]) % 4) + c) for x in range(4) for c in (0, 1)] for way in ((1, -1), (-1, 1)))


def params(mib):
    return pltpu.CompilerParams(vmem_limit_bytes=mib * 1024 * 1024)


def spread_kernel(states, out):
    for j in range(out.shape[0]):
        out[j] = states[:, :, DEPTH * j : DEPTH * (j + 1)].reshape(out.shape[1:])


def spread(states, mib):
    count = states.shape[0]
    return pl.pallas_call(
        spread_kernel,
        out_shape=jax.ShapeDtypeStruct((4, 2 * count, DEPTH), states.dtype),
        grid=(2,),
        in_specs=[pl.BlockSpec((count, 2, 2 * DEPTH), lambda g: (0, 0, g))],
        out_specs=pl.BlockSpec((2, 2 * count, DEPTH), lambda g: (g, 0, 0)),
        compiler_params=params(mib),
        name="spread",
    )(states)


def product_kernel(sizes, place, *refs):
    m = len(sizes)
    s_ref, (out, gg, tt, late, sem) = refs[m], refs[-5:]
    nt = (((1,), (1,)), ((), ()))
    starts = [sum(sizes[:i]) for i in range(m + 1)]
    held, copies = list(refs[:2]), [None, None]
    for i in range(2, m):
        held.append(late.at[pl.ds(starts[i] - starts[2], sizes[i])])
        copies.append(pltpu.make_async_copy(refs[i], held[i], sem.at[i - 2]))
    for copy in copies[2:]:
        copy.start()
    s = s_ref[...].reshape(192, DEPTH)
    ss = lax.dot_general(s, s, nt, preferred_element_type=F32)
    r = lax.broadcasted_iota(jnp.int32, (192, 192), 0)
    on = r == lax.broadcasted_iota(jnp.int32, (192, 192), 1)
    diag = jnp.sum(jnp.where(on, ss, 0.0), axis=0, keepdims=True)
    diag = jnp.broadcast_to(jnp.concatenate([diag, jnp.zeros((1, 64), F32)], axis=1), (8, 256))
    sub = lax.broadcasted_iota(jnp.int32, (8, 256), 0)
    lane8 = lax.broadcasted_iota(jnp.int32, (8, 256), 1)
    spare = jnp.zeros((8, 256), F32)
    for w in range(4):
        moved = pltpu.roll(diag, (SPARE + 1 - WINDOW * w) % 256, 1)
        spare = spare + jnp.where((sub == w) & (lane8 > SPARE), moved, 0.0)

    done = 0
    while done < m:
        last = done + 1
        while last < m and starts[last] - starts[done] < GROUP:
            last += 1
        a, n = starts[done], starts[last] - starts[done]
        for copy in copies[done:last]:
            if copy is not None:
                copy.wait()
        t = jnp.concatenate([ref[...] for ref in held[done:last]], axis=0).reshape(32 * n, DEPTH)
        done = last
        total = jnp.zeros((32 * n, 128), F32)
        for j in range(DEPTH // 128):
            x = t[:, 128 * j : 128 * j + 128].astype(F32)
            total = total + x * x
        at = pl.ds(32 * a, 32 * n)
        tt[at, :] = total
        even, odd = pl.ds(32 * a, 16 * n, stride=2), pl.ds(32 * a + 1, 16 * n, stride=2)
        tn = jnp.sum(tt[even, :] + tt[odd, :], axis=1, keepdims=True)
        lane = lax.broadcasted_iota(jnp.int32, (16 * n, 256), 1)
        first = lane % 2 == 0
        g = lax.dot_general(t, s, nt, preferred_element_type=F32)
        gg[0, at, :] = g[:, :128]
        gg[1, at, :] = jnp.concatenate([g[:, 128:], jnp.zeros((32 * n, 64), F32)], axis=1)
        gu, gv = (jnp.concatenate([gg[0, rows, :], gg[1, rows, :]], axis=1) for rows in (even, odd))
        both = gu + jnp.where(first, pltpu.roll(gv, 255, 1), -pltpu.roll(gv, 1, 1))
        both = jnp.where(lane < SPARE, both, jnp.where(lane == SPARE, tn, 0.0))
        both = (both.reshape(2 * n, 8, 256) + spare[None]).reshape(n, 2, 8, 256)
        for j in range(n):
            out[pl.ds(place[a + j], 1), pl.ds(place[sum(sizes) + a + j], 2)] = both[j : j + 1]


def products(at, blocks, s):
    n = len(at)
    place = jnp.stack([r for _, r, _ in at] + [4 * x + 2 * c for x, _, c in at]).astype(jnp.int32)
    out = pl.BlockSpec((4, 16, 8, 256), lambda k, place: (0, 0, 0, 0))
    return pl.pallas_call(
        functools.partial(product_kernel, [b.shape[0] for b in blocks]),
        out_shape=jax.ShapeDtypeStruct((4, 16, 8, 256), F32),
        grid_spec=pltpu.PrefetchScalarGridSpec(
            num_scalar_prefetch=1,
            grid=(1,),
            in_specs=[
                *[pl.BlockSpec(memory_space=pltpu.VMEM)] * 2,
                *[pl.BlockSpec(memory_space=pl.ANY)] * (len(blocks) - 2),
                pl.BlockSpec(memory_space=pltpu.VMEM),
            ],
            out_specs=out,
            scratch_shapes=[
                pltpu.VMEM((2, 32 * n, 128), F32),
                pltpu.VMEM((32 * n, 128), F32),
                pltpu.VMEM((n - blocks[0].shape[0] - blocks[1].shape[0], 32, DEPTH), jnp.bfloat16),
                pltpu.SemaphoreType.DMA((len(blocks) - 2,)),
            ],
        ),
        cost_estimate=pl.CostEstimate(flops=2 * 32 * n * 192 * DEPTH, bytes_accessed=64 * n * DEPTH, transcendentals=0),
        compiler_params=params(24),
        name="products",
    )(place, *blocks, s)


def per_device(train, test):
    a2a = functools.partial(lax.all_to_all, split_axis=0, concat_axis=0, tiled=True)
    x, core, row = lax.axis_index("x"), lax.axis_index("core"), lax.axis_index("row")
    held = spread(train, 60)
    t = a2a(held, "row")

    def swap(block):
        return lax.ppermute(block, "core", SWAP)

    def around(own):
        first = lax.ppermute(own, ("x", "core"), AHEAD)
        return first, lax.ppermute(own, ("x", "core"), BACK), lax.ppermute(first, ("x", "core"), AHEAD)

    stay = around(lax.dynamic_slice_in_dim(held, row, 1, 0))
    s, t, stay = lax.optimization_barrier((spread(test, 16), t, jnp.concatenate(stay)))
    s = a2a(s, "row")
    others = [(row + k) % 4 for k in (1, 2, 3)]
    come = around(jnp.concatenate([lax.dynamic_slice_in_dim(t, r, 1, 0) for r in others]))
    parts = [(t, range(4), (0,)), (stay, [row], (-1, 1, 2))] + [(b, others, (w,)) for b, w in zip(come, (-1, 1, 2))]
    entries = []
    for block, rows, ways in parts:
        for b, c, sign in ((block, core, 1 - 2 * core), (swap(block), 1 - core, 2 * core - 1)):
            entries.append((b, [((x + way * sign + 4) % 4, r, c) for way in ways for r in rows]))
    entries = [entries[i] for i in (0, 2, 1, 3, 4, 5, 6, 7, 8, 9)]
    blocks, at = [b for b, _ in entries], [place for _, places in entries for place in places]
    pieces = products(at, blocks, s)
    parts = a2a(pieces.reshape(64, 8, 256), ("row",) + DEV)
    total = jnp.sum(parts, axis=0)
    power = jnp.sum((total[:, :SPARE] ** 2).reshape(8, 96, 2), axis=2)
    tn = total[:, SPARE : SPARE + 1]
    diag = total[:4, SPARE + 1 :].reshape(4 * WINDOW)[:192]
    sn = jnp.sum(diag.reshape(1, 96, 2), axis=2)
    block = float(AMPS) * power / (tn * sn)
    full = a2a(jnp.broadcast_to(block[None], (16, 8, 96)), DEV)
    return full.reshape(128, 96)


def solution(mesh):
    axes = ("row", "x", "core", "zhi", "y")
    fine = Mesh(mesh.devices.reshape(4, 4, 2, 2, 8), axes)
    placed = (
        P(("row", "x", "core"), None, DEV),
        P(("x", "core", "row"), None, DEV),
    )
    return jax.shard_map(
        per_device, mesh=fine, in_specs=placed, out_specs=P("row", ("x", "core")), check_vma=False
    )
```

time: 140 us -> 138 us (0.986)
  the two profiles are of different devices: /device:TPU:2 before, /device:TPU:8 now
where the time goes in v4:
time: 138 us
  blocking collectives  48.5 us (35%)
  starting transfers between devices  42.3 us (31%)
  waiting for transfers between devices  31.4 us (23%)
  Pallas kernels  10.4 us (8%)
  local copies, waits for them, and re-layouts  2.45 us (2%)
  other arithmetic  2.39 us (2%)
    all_to_all x1, blocking collectives, per_device(): parts = a2a(pieces.reshape(64, 8, 256), ('row',) + DEV)  31.6 us
    all_to_all x1, blocking collectives, per_device(): full = a2a(jnp.broadcast_to(block[None], (16, 8, 96)), DEV)  16.8 us
    ppermute x5, starting transfers between devices, swap(): return lax.ppermute(block, 'core', SWAP)  10.6 us
    ppermute x2, waiting for transfers between devices, around(): first = lax.ppermute(own, ('x', 'core'), AHEAD)  9.45 us
    all_to_all x1, waiting for transfers between devices, per_device(): s = a2a(s, 'row')  8.86 us
    ppermute x2, waiting for transfers between devices, around(): lax.ppermute(first, ('x', 'core'), AHEAD)  8.46 us
    all_to_all x1, starting transfers between devices, per_device(): t = a2a(held, 'row')  7.39 us
    ppermute x2, starting transfers between devices, around(): lax.ppermute(own, ('x', 'core'), BACK)  7.31 us
  transfers between devices with their start and end apart: 13, of which 6 were waited for; matrix products, arithmetic and copies ran while one was open for 2% of the time, Pallas kernels for 1%

profile of v4, /device:TPU:8, one launch (start us, length us, event | category | flops | bytes accessed | tf_op | source)
XLA Modules:
  0.0 137.7 jit_solution(16168195757604086173)
XLA Ops:
  0.0 2.1 %spread.3 = bf16[4,32,4096]{2,1,0:T(8,128)(2,1)} custom-call(bf16[16,2,16384]{2,1,0:T(2,128)(2,1)} %states.3), custom_call_target="tpu_custom_call" | custom-call | tf_op jit(solution)/shard_map/spread/pallas_call | solution.py:33
  2.1 7.4 %all-to-all-start = ((bf16[4,32,4096]{2,1,0:T(8,128)(2,1)}), bf16[4,32,4096]{2,1,0:T(8,128)(2,1)S(1)}, u32[]{:S(2)}, u32[]{:S(2)}) async-start(bf16[4,32,4096]{2,1,0:T(8,128)(2,1)} %spread.3), calls=%async_computation | async-start | bytes 2097152 | tf_op jit(solution)/shard_map/all_to_all | solution.py:133
  10.4 3.4 %collective-permute-start = (bf16[1,32,4096]{2,1,0:T(8,128)(2,1)S(1)}, bf16[1,32,4096]{2,1,0:T(8,128)(2,1)S(1)}, u32[]{:S(2)}, u32[]{:S(2)}) collective-permute-start(bf16[1,32,4096]{2,1,0:T(8,128)(2,1)S(1)} %constant_dynamic-slice_fusion.3), channel_id=1, source_target_pairs={{0,32},{16,112},{32,64},{48,16},{64,96},{80,48},{96,0},{112,80},{1... | collective-permute-start | bytes 786440 | tf_op jit(solution)/shard_map/ppermute | solution.py:139
  13.8 3.7 %collective-permute-start.1 = (bf16[1,32,4096]{2,1,0:T(8,128)(2,1)S(1)}, bf16[1,32,4096]{2,1,0:T(8,128)(2,1)S(1)}, u32[]{:S(2)}, u32[]{:S(2)}) collective-permute-start(bf16[1,32,4096]{2,1,0:T(8,128)(2,1)S(1)} %constant_dynamic-slice_fusion.3), channel_id=1, source_target_pairs={{0,96},{16,48},{32,0},{48,80},{64,32},{80,112},{96,64},{112,16},{1... | collective-permute-start | bytes 786440 | tf_op jit(solution)/shard_map/ppermute | solution.py:140
  17.5 2.4 %collective-permute-done = bf16[1,32,4096]{2,1,0:T(8,128)(2,1)S(1)} collective-permute-done((bf16[1,32,4096]{2,1,0:T(8,128)(2,1)S(1)}, bf16[1,32,4096]{2,1,0:T(8,128)(2,1)S(1)}, u32[]{:S(2)}, u32[]{:S(2)}) %collective-permute-start) | collective-permute-done | bytes 262176 | tf_op jit(solution)/shard_map/ppermute | solution.py:139
  19.9 3.3 %collective-permute-start.2 = (bf16[1,32,4096]{2,1,0:T(8,128)(2,1)S(1)}, bf16[1,32,4096]{2,1,0:T(8,128)(2,1)}, u32[]{:S(2)}, u32[]{:S(2)}) collective-permute-start(bf16[1,32,4096]{2,1,0:T(8,128)(2,1)S(1)} %collective-permute-done), channel_id=1, source_target_pairs={{0,32},{16,112},{32,64},{48,16},{64,96},{80,48},{96,0},{112,80},{1... | collective-permute-start | bytes 786440 | tf_op jit(solution)/shard_map/ppermute | solution.py:140
  23.2 1.4 %spread.2 = bf16[4,48,4096]{2,1,0:T(8,128)(2,1)} custom-call(bf16[24,2,16384]{2,1,0:T(2,128)(2,1)S(1)} %copy-done), custom_call_target="tpu_custom_call" | custom-call | tf_op jit(solution)/shard_map/spread/pallas_call | solution.py:33
  24.6 4.9 %collective-permute-done.2 = bf16[1,32,4096]{2,1,0:T(8,128)(2,1)} collective-permute-done((bf16[1,32,4096]{2,1,0:T(8,128)(2,1)S(1)}, bf16[1,32,4096]{2,1,0:T(8,128)(2,1)}, u32[]{:S(2)}, u32[]{:S(2)}) %collective-permute-start.2) | collective-permute-done | bytes 262176 | tf_op jit(solution)/shard_map/ppermute | solution.py:140
  30.6 4.6 %all-to-all-done.refs_0_ = bf16[4,32,4096]{2,1,0:T(8,128)(2,1)S(1)} async-done(((bf16[4,32,4096]{2,1,0:T(8,128)(2,1)}), bf16[4,32,4096]{2,1,0:T(8,128)(2,1)S(1)}, u32[]{:S(2)}, u32[]{:S(2)}) %all-to-all-start) | async-done | bytes 1048608 | tf_op jit(solution)/shard_map/all_to_all | solution.py:133
  36.2 3.4 %collective-permute-start.5 = (bf16[3,32,4096]{2,1,0:T(8,128)(2,1)}, bf16[3,32,4096]{2,1,0:T(8,128)(2,1)}, u32[]{:S(2)}, u32[]{:S(2)}) collective-permute-start(bf16[3,32,4096]{2,1,0:T(8,128)(2,1)} %pad_maximum_fusion.1), channel_id=1, source_target_pairs={{0,32},{16,112},{32,64},{48,16},{64,96},{80,48},{96,0},{112,80},{1... | collective-permute-start | bytes 2359304 | tf_op jit(solution)/shard_map/ppermute | solution.py:139
  39.6 3.6 %all-to-all-start.1 = ((bf16[4,48,4096]{2,1,0:T(8,128)(2,1)}), bf16[4,48,4096]{2,1,0:T(8,128)(2,1)S(1)}, u32[]{:S(2)}, u32[]{:S(2)}) async-start(bf16[4,48,4096]{2,1,0:T(8,128)(2,1)} %spread.2), calls=%async_computation.1 | async-start | bytes 3145728 | tf_op jit(solution)/shard_map/all_to_all | solution.py:144
  43.2 3.7 %collective-permute-start.7 = (bf16[3,32,4096]{2,1,0:T(8,128)(2,1)}, bf16[3,32,4096]{2,1,0:T(8,128)(2,1)}, u32[]{:S(2)}, u32[]{:S(2)}) collective-permute-start(bf16[3,32,4096]{2,1,0:T(8,128)(2,1)} %pad_maximum_fusion.1), channel_id=1, source_target_pairs={{0,96},{16,48},{32,0},{48,80},{64,32},{80,112},{96,64},{112,16},{1... | collective-permute-start | bytes 2359304 | tf_op jit(solution)/shard_map/ppermute | solution.py:140
  46.9 7.0 %collective-permute-done.5.refs_4_ = bf16[3,32,4096]{2,1,0:T(8,128)(2,1)} collective-permute-done((bf16[3,32,4096]{2,1,0:T(8,128)(2,1)}, bf16[3,32,4096]{2,1,0:T(8,128)(2,1)}, u32[]{:S(2)}, u32[]{:S(2)}) %collective-permute-start.5) | collective-permute-done | bytes 786464 | tf_op jit(solution)/shard_map/ppermute | solution.py:139
  53.9 3.4 %collective-permute-start.9 = (bf16[3,32,4096]{2,1,0:T(8,128)(2,1)}, bf16[3,32,4096]{2,1,0:T(8,128)(2,1)}, u32[]{:S(2)}, u32[]{:S(2)}) collective-permute-start(bf16[3,32,4096]{2,1,0:T(8,128)(2,1)} %collective-permute-done.5.refs_4_), channel_id=1, source_target_pairs={{0,32},{16,112},{32,64},{48,16},{64,96},{80,48},{96,0},{112,80},{1... | collective-permute-start | bytes 2359304 | tf_op jit(solution)/shard_map/ppermute | solution.py:140
  57.3 1.9 %collective-permute-start.3 = (bf16[4,32,4096]{2,1,0:T(8,128)(2,1)S(1)}, bf16[4,32,4096]{2,1,0:T(8,128)(2,1)}, u32[]{:S(2)}, u32[]{:S(2)}) collective-permute-start(bf16[4,32,4096]{2,1,0:T(8,128)(2,1)S(1)} %all-to-all-done.refs_0_), channel_id=1, source_target_pairs={{0,16},{16,0},{1,17},{17,1},{2,18},{18,2},{3,19},{19,3},{4,20},{20... | collective-permute-start | bytes 3145736 | tf_op jit(solution)/shard_map/ppermute | solution.py:136
  59.3 2.4 %collective-permute-start.4 = (bf16[3,32,4096]{2,1,0:T(8,128)(2,1)S(1)}, bf16[3,32,4096]{2,1,0:T(8,128)(2,1)}, u32[]{:S(2)}, u32[]{:S(2)}) collective-permute-start(bf16[3,32,4096]{2,1,0:T(8,128)(2,1)S(1)} %pad_maximum_fusion.refs_1_), channel_id=1, source_target_pairs={{0,16},{16,0},{1,17},{17,1},{2,18},{18,2},{3,19},{19,3},{4,20},{20... | collective-permute-start | bytes 2359304 | tf_op jit(solution)/shard_map/ppermute | solution.py:136
  61.7 1.9 %collective-permute-start.8 = (bf16[3,32,4096]{2,1,0:T(8,128)(2,1)}, bf16[3,32,4096]{2,1,0:T(8,128)(2,1)}, u32[]{:S(2)}, u32[]{:S(2)}) collective-permute-start(bf16[3,32,4096]{2,1,0:T(8,128)(2,1)} %collective-permute-done.7.refs_6_), channel_id=1, source_target_pairs={{0,16},{16,0},{1,17},{17,1},{2,18},{18,2},{3,19},{19,3},{4,20},{20... | collective-permute-start | bytes 2359304 | tf_op jit(solution)/shard_map/ppermute | solution.py:136
  63.6 2.4 %collective-permute-start.6 = (bf16[3,32,4096]{2,1,0:T(8,128)(2,1)}, bf16[3,32,4096]{2,1,0:T(8,128)(2,1)}, u32[]{:S(2)}, u32[]{:S(2)}) collective-permute-start(bf16[3,32,4096]{2,1,0:T(8,128)(2,1)} %collective-permute-done.5.refs_4_), channel_id=1, source_target_pairs={{0,16},{16,0},{1,17},{17,1},{2,18},{18,2},{3,19},{19,3},{4,20},{20... | collective-permute-start | bytes 2359304 | tf_op jit(solution)/shard_map/ppermute | solution.py:136
  66.0 3.5 %collective-permute-done.9.refs_8_ = bf16[3,32,4096]{2,1,0:T(8,128)(2,1)} collective-permute-done((bf16[3,32,4096]{2,1,0:T(8,128)(2,1)}, bf16[3,32,4096]{2,1,0:T(8,128)(2,1)}, u32[]{:S(2)}, u32[]{:S(2)}) %collective-permute-start.9) | collective-permute-done | bytes 786464 | tf_op jit(solution)/shard_map/ppermute | solution.py:140
  69.6 1.9 %collective-permute-start.10 = (bf16[3,32,4096]{2,1,0:T(8,128)(2,1)}, bf16[3,32,4096]{2,1,0:T(8,128)(2,1)}, u32[]{:S(2)}, u32[]{:S(2)}) collective-permute-start(bf16[3,32,4096]{2,1,0:T(8,128)(2,1)} %collective-permute-done.9.refs_8_), channel_id=1, source_target_pairs={{0,16},{16,0},{1,17},{17,1},{2,18},{18,2},{3,19},{19,3},{4,20},{20... | collective-permute-start | bytes 2359304 | tf_op jit(solution)/shard_map/ppermute | solution.py:136
  71.8 8.9 %all-to-all-done.1.refs_10_ = bf16[4,48,4096]{2,1,0:T(8,128)(2,1)S(1)} async-done(((bf16[4,48,4096]{2,1,0:T(8,128)(2,1)}), bf16[4,48,4096]{2,1,0:T(8,128)(2,1)S(1)}, u32[]{:S(2)}, u32[]{:S(2)}) %all-to-all-start.1) | async-done | bytes 1572896 | tf_op jit(solution)/shard_map/all_to_all | solution.py:144
  80.6 6.9 %products.1 = f32[4,16,8,256]{3,2,1,0:T(8,128)S(1)} custom-call(s32[64]{0:T(128)S(1)} %stack.38.place, bf16[4,32,4096]{2,1,0:T(8,128)(2,1)S(1)} %all-to-all-done.refs_0_, bf16[3,32,4096]{2,1,0:T(8,128)(2,1)S(1)} %pad_maximum_fusion.refs_1_, bf16[4,32,4096]{2,1,0:T(8,128)(2,1)} %collective-permute-done.3.refs_2_, ...), custom_call_target="tpu_custom_call" | custom-call | flops 1610612736 | bytes 8388608 | tf_op jit(solution)/shard_map/products/pallas_call | solution.py:104
  87.5 31.6 %all_to_all.20 = f32[64,8,256]{2,1,0:T(8,128)S(1)} all-to-all(f32[64,8,256]{2,1,0:T(8,128)S(1)} %bitcast.15), channel_id=1, replica_groups=mesh['row'=4,'x'=4,'core'=2,'zhi'=2,'y'=8] {'row','zhi','y'}, dimensions={0} | all-to-all | bytes 1048576 | tf_op jit(solution)/shard_map/all_to_all | solution.py:155
  120.2 16.8 %all_to_all.21 = f32[16,8,96]{2,1,0:T(8,128)S(1)} all-to-all(f32[16,8,96]{2,1,0:T(8,128)S(1)} %broadcast_in_dim.2), channel_id=1, replica_groups=mesh['row'=4,'x'=4,'core'=2,'zhi'=2,'y'=8] {'zhi','y'}, dimensions={0} | all-to-all | bytes 98304 | tf_op jit(solution)/shard_map/all_to_all | solution.py:162
  (26 shorter events, 4.9 us)
Async XLA Ops:
  2.1 21.2 %copy-start = (bf16[24,2,16384]{2,1,0:T(2,128)(2,1)S(1)}, bf16[24,2,16384]{2,1,0:T(2,128)(2,1)}, u32[]{:S(2)}) copy-start(bf16[24,2,16384]{2,1,0:T(2,128)(2,1)} %states.2) | copy-start | bytes 4718596
  2.1 33.1 %all-to-all-start = ((bf16[4,32,4096]{2,1,0:T(8,128)(2,1)}), bf16[4,32,4096]{2,1,0:T(8,128)(2,1)S(1)}, u32[]{:S(2)}, u32[]{:S(2)}) async-start(bf16[4,32,4096]{2,1,0:T(8,128)(2,1)} %spread.3), calls=%async_computation | async-start | bytes 2097152 | tf_op jit(solution)/shard_map/all_to_all | solution.py:133
  10.4 9.5 %collective-permute-start = (bf16[1,32,4096]{2,1,0:T(8,128)(2,1)S(1)}, bf16[1,32,4096]{2,1,0:T(8,128)(2,1)S(1)}, u32[]{:S(2)}, u32[]{:S(2)}) collective-permute-start(bf16[1,32,4096]{2,1,0:T(8,128)(2,1)S(1)} %constant_dynamic-slice_fusion.3), channel_id=1, source_target_pairs={{0,32},{16,112},{32,64},{48,16},{64,96},{80,48},{96,0},{112,80},{1... | collective-permute-start | bytes 786440 | tf_op jit(solution)/shard_map/ppermute | solution.py:139
  13.8 10.8 %collective-permute-start.1 = (bf16[1,32,4096]{2,1,0:T(8,128)(2,1)S(1)}, bf16[1,32,4096]{2,1,0:T(8,128)(2,1)S(1)}, u32[]{:S(2)}, u32[]{:S(2)}) collective-permute-start(bf16[1,32,4096]{2,1,0:T(8,128)(2,1)S(1)} %constant_dynamic-slice_fusion.3), channel_id=1, source_target_pairs={{0,96},{16,48},{32,0},{48,80},{64,32},{80,112},{96,64},{112,16},{1... | collective-permute-start | bytes 786440 | tf_op jit(solution)/shard_map/ppermute | solution.py:140
  19.9 9.6 %collective-permute-start.2 = (bf16[1,32,4096]{2,1,0:T(8,128)(2,1)S(1)}, bf16[1,32,4096]{2,1,0:T(8,128)(2,1)}, u32[]{:S(2)}, u32[]{:S(2)}) collective-permute-start(bf16[1,32,4096]{2,1,0:T(8,128)(2,1)S(1)} %collective-permute-done), channel_id=1, source_target_pairs={{0,32},{16,112},{32,64},{48,16},{64,96},{80,48},{96,0},{112,80},{1... | collective-permute-start | bytes 786440 | tf_op jit(solution)/shard_map/ppermute | solution.py:140
  36.2 17.7 %collective-permute-start.5 = (bf16[3,32,4096]{2,1,0:T(8,128)(2,1)}, bf16[3,32,4096]{2,1,0:T(8,128)(2,1)}, u32[]{:S(2)}, u32[]{:S(2)}) collective-permute-start(bf16[3,32,4096]{2,1,0:T(8,128)(2,1)} %pad_maximum_fusion.1), channel_id=1, source_target_pairs={{0,32},{16,112},{32,64},{48,16},{64,96},{80,48},{96,0},{112,80},{1... | collective-permute-start | bytes 2359304 | tf_op jit(solution)/shard_map/ppermute | solution.py:139
  39.6 41.0 %all-to-all-start.1 = ((bf16[4,48,4096]{2,1,0:T(8,128)(2,1)}), bf16[4,48,4096]{2,1,0:T(8,128)(2,1)S(1)}, u32[]{:S(2)}, u32[]{:S(2)}) async-start(bf16[4,48,4096]{2,1,0:T(8,128)(2,1)} %spread.2), calls=%async_computation.1 | async-start | bytes 3145728 | tf_op jit(solution)/shard_map/all_to_all | solution.py:144
  43.2 18.5 %collective-permute-start.7 = (bf16[3,32,4096]{2,1,0:T(8,128)(2,1)}, bf16[3,32,4096]{2,1,0:T(8,128)(2,1)}, u32[]{:S(2)}, u32[]{:S(2)}) collective-permute-start(bf16[3,32,4096]{2,1,0:T(8,128)(2,1)} %pad_maximum_fusion.1), channel_id=1, source_target_pairs={{0,96},{16,48},{32,0},{48,80},{64,32},{80,112},{96,64},{112,16},{1... | collective-permute-start | bytes 2359304 | tf_op jit(solution)/shard_map/ppermute | solution.py:140
  53.9 15.7 %collective-permute-start.9 = (bf16[3,32,4096]{2,1,0:T(8,128)(2,1)}, bf16[3,32,4096]{2,1,0:T(8,128)(2,1)}, u32[]{:S(2)}, u32[]{:S(2)}) collective-permute-start(bf16[3,32,4096]{2,1,0:T(8,128)(2,1)} %collective-permute-done.5.refs_4_), channel_id=1, source_target_pairs={{0,32},{16,112},{32,64},{48,16},{64,96},{80,48},{96,0},{112,80},{1... | collective-permute-start | bytes 2359304 | tf_op jit(solution)/shard_map/ppermute | solution.py:140
  57.3 14.4 %collective-permute-start.3 = (bf16[4,32,4096]{2,1,0:T(8,128)(2,1)S(1)}, bf16[4,32,4096]{2,1,0:T(8,128)(2,1)}, u32[]{:S(2)}, u32[]{:S(2)}) collective-permute-start(bf16[4,32,4096]{2,1,0:T(8,128)(2,1)S(1)} %all-to-all-done.refs_0_), channel_id=1, source_target_pairs={{0,16},{16,0},{1,17},{17,1},{2,18},{18,2},{3,19},{19,3},{4,20},{20... | collective-permute-start | bytes 3145736 | tf_op jit(solution)/shard_map/ppermute | solution.py:136
  59.3 12.5 %collective-permute-start.4 = (bf16[3,32,4096]{2,1,0:T(8,128)(2,1)S(1)}, bf16[3,32,4096]{2,1,0:T(8,128)(2,1)}, u32[]{:S(2)}, u32[]{:S(2)}) collective-permute-start(bf16[3,32,4096]{2,1,0:T(8,128)(2,1)S(1)} %pad_maximum_fusion.refs_1_), channel_id=1, source_target_pairs={{0,16},{16,0},{1,17},{17,1},{2,18},{18,2},{3,19},{19,3},{4,20},{20... | collective-permute-start | bytes 2359304 | tf_op jit(solution)/shard_map/ppermute | solution.py:136
  61.7 10.1 %collective-permute-start.8 = (bf16[3,32,4096]{2,1,0:T(8,128)(2,1)}, bf16[3,32,4096]{2,1,0:T(8,128)(2,1)}, u32[]{:S(2)}, u32[]{:S(2)}) collective-permute-start(bf16[3,32,4096]{2,1,0:T(8,128)(2,1)} %collective-permute-done.7.refs_6_), channel_id=1, source_target_pairs={{0,16},{16,0},{1,17},{17,1},{2,18},{18,2},{3,19},{19,3},{4,20},{20... | collective-permute-start | bytes 2359304 | tf_op jit(solution)/shard_map/ppermute | solution.py:136
  63.6 8.1 %collective-permute-start.6 = (bf16[3,32,4096]{2,1,0:T(8,128)(2,1)}, bf16[3,32,4096]{2,1,0:T(8,128)(2,1)}, u32[]{:S(2)}, u32[]{:S(2)}) collective-permute-start(bf16[3,32,4096]{2,1,0:T(8,128)(2,1)} %collective-permute-done.5.refs_4_), channel_id=1, source_target_pairs={{0,16},{16,0},{1,17},{17,1},{2,18},{18,2},{3,19},{19,3},{4,20},{20... | collective-permute-start | bytes 2359304 | tf_op jit(solution)/shard_map/ppermute | solution.py:136
  69.6 11.1 %collective-permute-start.10 = (bf16[3,32,4096]{2,1,0:T(8,128)(2,1)}, bf16[3,32,4096]{2,1,0:T(8,128)(2,1)}, u32[]{:S(2)}, u32[]{:S(2)}) collective-permute-start(bf16[3,32,4096]{2,1,0:T(8,128)(2,1)} %collective-permute-done.9.refs_8_), channel_id=1, source_target_pairs={{0,16},{16,0},{1,17},{17,1},{2,18},{18,2},{3,19},{19,3},{4,20},{20... | collective-permute-start | bytes 2359304 | tf_op jit(solution)/shard_map/ppermute | solution.py:136

commit v5 on v4

--- a/solution.py
+++ b/solution.py
@@ -152,14 +152,15 @@
     entries = [entries[i] for i in (0, 2, 1, 3, 4, 5, 6, 7, 8, 9)]
     blocks, at = [b for b, _ in entries], [place for _, places in entries for place in places]
     pieces = products(at, blocks, s)
-    parts = a2a(pieces.reshape(64, 8, 256), ("row",) + DEV)
+    parts = a2a(pieces.reshape(32, 16, 256), ("row", "y"))
     total = jnp.sum(parts, axis=0)
-    power = jnp.sum((total[:, :SPARE] ** 2).reshape(8, 96, 2), axis=2)
+    total = total + lax.ppermute(total, "zhi", SWAP)
+    power = jnp.sum((total[:, :SPARE] ** 2).reshape(16, 96, 2), axis=2)
     tn = total[:, SPARE : SPARE + 1]
     diag = total[:4, SPARE + 1 :].reshape(4 * WINDOW)[:192]
     sn = jnp.sum(diag.reshape(1, 96, 2), axis=2)
     block = float(AMPS) * power / (tn * sn)
-    full = a2a(jnp.broadcast_to(block[None], (16, 8, 96)), DEV)
+    full = a2a(jnp.broadcast_to(block[None], (8, 16, 96)), "y")
     return full.reshape(128, 96)
 
 

time: 138 us -> 136 us (0.986)
  blocking collectives: 48.5 us -> 36 us
  starting transfers between devices: 42.3 us -> 50.5 us
  waiting for transfers between devices: 31.4 us -> 33.1 us
    all_to_all x2, blocking collectives: 48.5 us -> 36 us  [the longest x1 25.3 us: per_device(): parts = a2a(pieces.reshape(32, 16, 256), ('row', 'y'))]
    ppermute x0 -> x1, starting transfers between devices: none -> 8.23 us  [per_device(): total = total + lax.ppermute(total, 'zhi', SWAP)]
    ppermute x0 -> x1, waiting for transfers between devices: none -> 1.7 us  [per_device(): total = total + lax.ppermute(total, 'zhi', SWAP)]
  transfers between devices with their start and end apart: 13 -> 14, of which waited for: 6 -> 7; matrix products, arithmetic and copies ran while one was open for 2% -> 2% of each run, Pallas kernels for 1% -> 1%
where the time goes in v5:
time: 136 us; the launch traced here: 135 us
  starting transfers between devices  50.5 us (37%)
  blocking collectives  36 us (26%)
  waiting for transfers between devices  33.1 us (24%)
  Pallas kernels  10.4 us (8%)
  local copies, waits for them, and re-layouts  2.44 us (2%)
  other arithmetic  2.37 us (2%)
    all_to_all x1, blocking collectives, per_device(): parts = a2a(pieces.reshape(32, 16, 256), ('row', 'y'))  25.3 us
    all_to_all x1, blocking collectives, per_device(): full = a2a(jnp.broadcast_to(block[None], (8, 16, 96)), 'y')  10.7 us
    ppermute x5, starting transfers between devices, swap(): return lax.ppermute(block, 'core', SWAP)  10.6 us
    ppermute x2, waiting for transfers between devices, around(): first = lax.ppermute(own, ('x', 'core'), AHEAD)  9.45 us
    all_to_all x1, waiting for transfers between devices, per_device(): s = a2a(s, 'row')  8.86 us
    ppermute x2, waiting for transfers between devices, around(): lax.ppermute(first, ('x', 'core'), AHEAD)  8.46 us
    ppermute x1, starting transfers between devices, per_device(): total = total + lax.ppermute(total, 'zhi', SWAP)  8.23 us
    all_to_all x1, starting transfers between devices, per_device(): t = a2a(held, 'row')  7.39 us
  transfers between devices with their start and end apart: 14, of which 7 were waited for; matrix products, arithmetic and copies ran while one was open for 2% of the time, Pallas kernels for 1%

profile of v5, /device:TPU:8, one launch (start us, length us, event | category | flops | bytes accessed | tf_op | source)
XLA Modules:
  0.0 135.1 jit_solution(1331042360061516992)
XLA Ops:
  0.0 2.1 %spread.3 = bf16[4,32,4096]{2,1,0:T(8,128)(2,1)} custom-call(bf16[16,2,16384]{2,1,0:T(2,128)(2,1)} %states.3), custom_call_target="tpu_custom_call" | custom-call | tf_op jit(solution)/shard_map/spread/pallas_call | solution.py:33
  2.1 7.4 %all-to-all-start = ((bf16[4,32,4096]{2,1,0:T(8,128)(2,1)}), bf16[4,32,4096]{2,1,0:T(8,128)(2,1)S(1)}, u32[]{:S(2)}, u32[]{:S(2)}) async-start(bf16[4,32,4096]{2,1,0:T(8,128)(2,1)} %spread.3), calls=%async_computation | async-start | bytes 2097152 | tf_op jit(solution)/shard_map/all_to_all | solution.py:133
  10.4 3.4 %collective-permute-start = (bf16[1,32,4096]{2,1,0:T(8,128)(2,1)S(1)}, bf16[1,32,4096]{2,1,0:T(8,128)(2,1)S(1)}, u32[]{:S(2)}, u32[]{:S(2)}) collective-permute-start(bf16[1,32,4096]{2,1,0:T(8,128)(2,1)S(1)} %constant_dynamic-slice_fusion.3), channel_id=1, source_target_pairs={{0,32},{16,112},{32,64},{48,16},{64,96},{80,48},{96,0},{112,80},{1... | collective-permute-start | bytes 786440 | tf_op jit(solution)/shard_map/ppermute | solution.py:139
  13.9 3.7 %collective-permute-start.1 = (bf16[1,32,4096]{2,1,0:T(8,128)(2,1)S(1)}, bf16[1,32,4096]{2,1,0:T(8,128)(2,1)S(1)}, u32[]{:S(2)}, u32[]{:S(2)}) collective-permute-start(bf16[1,32,4096]{2,1,0:T(8,128)(2,1)S(1)} %constant_dynamic-slice_fusion.3), channel_id=1, source_target_pairs={{0,96},{16,48},{32,0},{48,80},{64,32},{80,112},{96,64},{112,16},{1... | collective-permute-start | bytes 786440 | tf_op jit(solution)/shard_map/ppermute | solution.py:140
  17.5 2.4 %collective-permute-done = bf16[1,32,4096]{2,1,0:T(8,128)(2,1)S(1)} collective-permute-done((bf16[1,32,4096]{2,1,0:T(8,128)(2,1)S(1)}, bf16[1,32,4096]{2,1,0:T(8,128)(2,1)S(1)}, u32[]{:S(2)}, u32[]{:S(2)}) %collective-permute-start) | collective-permute-done | bytes 262176 | tf_op jit(solution)/shard_map/ppermute | solution.py:139
  19.9 3.3 %collective-permute-start.2 = (bf16[1,32,4096]{2,1,0:T(8,128)(2,1)S(1)}, bf16[1,32,4096]{2,1,0:T(8,128)(2,1)}, u32[]{:S(2)}, u32[]{:S(2)}) collective-permute-start(bf16[1,32,4096]{2,1,0:T(8,128)(2,1)S(1)} %collective-permute-done), channel_id=1, source_target_pairs={{0,32},{16,112},{32,64},{48,16},{64,96},{80,48},{96,0},{112,80},{1... | collective-permute-start | bytes 786440 | tf_op jit(solution)/shard_map/ppermute | solution.py:140
  24.6 4.9 %collective-permute-done.2 = bf16[1,32,4096]{2,1,0:T(8,128)(2,1)} collective-permute-done((bf16[1,32,4096]{2,1,0:T(8,128)(2,1)S(1)}, bf16[1,32,4096]{2,1,0:T(8,128)(2,1)}, u32[]{:S(2)}, u32[]{:S(2)}) %collective-permute-start.2) | collective-permute-done | bytes 262176 | tf_op jit(solution)/shard_map/ppermute | solution.py:140
  30.6 4.6 %all-to-all-done.refs_0_ = bf16[4,32,4096]{2,1,0:T(8,128)(2,1)S(1)} async-done(((bf16[4,32,4096]{2,1,0:T(8,128)(2,1)}), bf16[4,32,4096]{2,1,0:T(8,128)(2,1)S(1)}, u32[]{:S(2)}, u32[]{:S(2)}) %all-to-all-start) | async-done | bytes 1048608 | tf_op jit(solution)/shard_map/all_to_all | solution.py:133
  36.2 3.4 %collective-permute-start.5 = (bf16[3,32,4096]{2,1,0:T(8,128)(2,1)}, bf16[3,32,4096]{2,1,0:T(8,128)(2,1)}, u32[]{:S(2)}, u32[]{:S(2)}) collective-permute-start(bf16[3,32,4096]{2,1,0:T(8,128)(2,1)} %pad_maximum_fusion.1), channel_id=1, source_target_pairs={{0,32},{16,112},{32,64},{48,16},{64,96},{80,48},{96,0},{112,80},{1... | collective-permute-start | bytes 2359304 | tf_op jit(solution)/shard_map/ppermute | solution.py:139
  39.6 3.6 %all-to-all-start.1 = ((bf16[4,48,4096]{2,1,0:T(8,128)(2,1)}), bf16[4,48,4096]{2,1,0:T(8,128)(2,1)S(1)}, u32[]{:S(2)}, u32[]{:S(2)}) async-start(bf16[4,48,4096]{2,1,0:T(8,128)(2,1)} %spread.2), calls=%async_computation.1 | async-start | bytes 3145728 | tf_op jit(solution)/shard_map/all_to_all | solution.py:144
  43.2 3.7 %collective-permute-start.7 = (bf16[3,32,4096]{2,1,0:T(8,128)(2,1)}, bf16[3,32,4096]{2,1,0:T(8,128)(2,1)}, u32[]{:S(2)}, u32[]{:S(2)}) collective-permute-start(bf16[3,32,4096]{2,1,0:T(8,128)(2,1)} %pad_maximum_fusion.1), channel_id=1, source_target_pairs={{0,96},{16,48},{32,0},{48,80},{64,32},{80,112},{96,64},{112,16},{1... | collective-permute-start | bytes 2359304 | tf_op jit(solution)/shard_map/ppermute | solution.py:140
  46.9 7.0 %collective-permute-done.5.refs_4_ = bf16[3,32,4096]{2,1,0:T(8,128)(2,1)} collective-permute-done((bf16[3,32,4096]{2,1,0:T(8,128)(2,1)}, bf16[3,32,4096]{2,1,0:T(8,128)(2,1)}, u32[]{:S(2)}, u32[]{:S(2)}) %collective-permute-start.5) | collective-permute-done | bytes 786464 | tf_op jit(solution)/shard_map/ppermute | solution.py:139
  53.9 3.4 %collective-permute-start.9 = (bf16[3,32,4096]{2,1,0:T(8,128)(2,1)}, bf16[3,32,4096]{2,1,0:T(8,128)(2,1)}, u32[]{:S(2)}, u32[]{:S(2)}) collective-permute-start(bf16[3,32,4096]{2,1,0:T(8,128)(2,1)} %collective-permute-done.5.refs_4_), channel_id=1, source_target_pairs={{0,32},{16,112},{32,64},{48,16},{64,96},{80,48},{96,0},{112,80},{1... | collective-permute-start | bytes 2359304 | tf_op jit(solution)/shard_map/ppermute | solution.py:140
  57.3 1.9 %collective-permute-start.3 = (bf16[4,32,4096]{2,1,0:T(8,128)(2,1)S(1)}, bf16[4,32,4096]{2,1,0:T(8,128)(2,1)}, u32[]{:S(2)}, u32[]{:S(2)}) collective-permute-start(bf16[4,32,4096]{2,1,0:T(8,128)(2,1)S(1)} %all-to-all-done.refs_0_), channel_id=1, source_target_pairs={{0,16},{16,0},{1,17},{17,1},{2,18},{18,2},{3,19},{19,3},{4,20},{20... | collective-permute-start | bytes 3145736 | tf_op jit(solution)/shard_map/ppermute | solution.py:136
  59.3 2.4 %collective-permute-start.4 = (bf16[3,32,4096]{2,1,0:T(8,128)(2,1)S(1)}, bf16[3,32,4096]{2,1,0:T(8,128)(2,1)}, u32[]{:S(2)}, u32[]{:S(2)}) collective-permute-start(bf16[3,32,4096]{2,1,0:T(8,128)(2,1)S(1)} %pad_maximum_fusion.refs_1_), channel_id=1, source_target_pairs={{0,16},{16,0},{1,17},{17,1},{2,18},{18,2},{3,19},{19,3},{4,20},{20... | collective-permute-start | bytes 2359304 | tf_op jit(solution)/shard_map/ppermute | solution.py:136
  61.7 1.9 %collective-permute-start.8 = (bf16[3,32,4096]{2,1,0:T(8,128)(2,1)}, bf16[3,32,4096]{2,1,0:T(8,128)(2,1)}, u32[]{:S(2)}, u32[]{:S(2)}) collective-permute-start(bf16[3,32,4096]{2,1,0:T(8,128)(2,1)} %collective-permute-done.7.refs_6_), channel_id=1, source_target_pairs={{0,16},{16,0},{1,17},{17,1},{2,18},{18,2},{3,19},{19,3},{4,20},{20... | collective-permute-start | bytes 2359304 | tf_op jit(solution)/shard_map/ppermute | solution.py:136
  63.6 2.4 %collective-permute-start.6 = (bf16[3,32,4096]{2,1,0:T(8,128)(2,1)}, bf16[3,32,4096]{2,1,0:T(8,128)(2,1)}, u32[]{:S(2)}, u32[]{:S(2)}) collective-permute-start(bf16[3,32,4096]{2,1,0:T(8,128)(2,1)} %collective-permute-done.5.refs_4_), channel_id=1, source_target_pairs={{0,16},{16,0},{1,17},{17,1},{2,18},{18,2},{3,19},{19,3},{4,20},{20... | collective-permute-start | bytes 2359304 | tf_op jit(solution)/shard_map/ppermute | solution.py:136
  66.0 3.5 %collective-permute-done.9.refs_8_ = bf16[3,32,4096]{2,1,0:T(8,128)(2,1)} collective-permute-done((bf16[3,32,4096]{2,1,0:T(8,128)(2,1)}, bf16[3,32,4096]{2,1,0:T(8,128)(2,1)}, u32[]{:S(2)}, u32[]{:S(2)}) %collective-permute-start.9) | collective-permute-done | bytes 786464 | tf_op jit(solution)/shard_map/ppermute | solution.py:140
  69.6 1.9 %collective-permute-start.10 = (bf16[3,32,4096]{2,1,0:T(8,128)(2,1)}, bf16[3,32,4096]{2,1,0:T(8,128)(2,1)}, u32[]{:S(2)}, u32[]{:S(2)}) collective-permute-start(bf16[3,32,4096]{2,1,0:T(8,128)(2,1)} %collective-permute-done.9.refs_8_), channel_id=1, source_target_pairs={{0,16},{16,0},{1,17},{17,1},{2,18},{18,2},{3,19},{19,3},{4,20},{20... | collective-permute-start | bytes 2359304 | tf_op jit(solution)/shard_map/ppermute | solution.py:136
  71.8 8.9 %all-to-all-done.1.refs_10_ = bf16[4,48,4096]{2,1,0:T(8,128)(2,1)S(1)} async-done(((bf16[4,48,4096]{2,1,0:T(8,128)(2,1)}), bf16[4,48,4096]{2,1,0:T(8,128)(2,1)S(1)}, u32[]{:S(2)}, u32[]{:S(2)}) %all-to-all-start.1) | async-done | bytes 1572896 | tf_op jit(solution)/shard_map/all_to_all | solution.py:144
  80.6 6.9 %products.1 = f32[4,16,8,256]{3,2,1,0:T(8,128)S(1)} custom-call(s32[64]{0:T(128)S(1)} %stack.38.place, bf16[4,32,4096]{2,1,0:T(8,128)(2,1)S(1)} %all-to-all-done.refs_0_, bf16[3,32,4096]{2,1,0:T(8,128)(2,1)S(1)} %pad_maximum_fusion.refs_1_, bf16[4,32,4096]{2,1,0:T(8,128)(2,1)} %collective-permute-done.3.refs_2_, ...), custom_call_target="tpu_custom_call" | custom-call | flops 1610612736 | bytes 8388608 | tf_op jit(solution)/shard_map/products/pallas_call | solution.py:104
  87.6 25.3 %all_to_all.20 = f32[32,16,256]{2,1,0:T(8,128)S(1)} all-to-all(f32[32,16,256]{2,1,0:T(8,128)S(1)} %bitcast.15), channel_id=1, replica_groups=mesh['row'=4,'x'=4,'core'=2,'zhi'=2,'y'=8] {'row','y'}, dimensions={0} | all-to-all | bytes 1048576 | tf_op jit(solution)/shard_map/all_to_all | solution.py:155
  112.9 8.2 %collective-permute-start.11 = (f32[16,256]{1,0:T(8,128)S(1)}, f32[16,256]{1,0:T(8,128)S(1)}, u32[]{:S(2)}, u32[]{:S(2)}) collective-permute-start(f32[16,256]{1,0:T(8,128)S(1)} %reduce_sum.27), channel_id=1, source_target_pairs={{0,8},{8,0},{1,9},{9,1},{2,10},{10,2},{3,11},{11,3},{4,12},{12,4},... | collective-permute-start | bytes 49160 | tf_op jit(solution)/shard_map/ppermute | solution.py:157
  123.8 10.7 %all_to_all.21 = f32[8,16,96]{2,1,0:T(8,128)S(1)} all-to-all(f32[8,16,96]{2,1,0:T(8,128)S(1)} %broadcast_in_dim.2), channel_id=1, replica_groups=mesh['row'=4,'x'=4,'core'=2,'zhi'=2,'y'=8] {'y'}, dimensions={0} | all-to-all | bytes 98304 | tf_op jit(solution)/shard_map/all_to_all | solution.py:163
  (29 shorter events, 7.9 us)
Async XLA Ops:
  2.1 21.2 %copy-start = (bf16[24,2,16384]{2,1,0:T(2,128)(2,1)S(1)}, bf16[24,2,16384]{2,1,0:T(2,128)(2,1)}, u32[]{:S(2)}) copy-start(bf16[24,2,16384]{2,1,0:T(2,128)(2,1)} %states.2) | copy-start | bytes 4718596
  2.1 33.1 %all-to-all-start = ((bf16[4,32,4096]{2,1,0:T(8,128)(2,1)}), bf16[4,32,4096]{2,1,0:T(8,128)(2,1)S(1)}, u32[]{:S(2)}, u32[]{:S(2)}) async-start(bf16[4,32,4096]{2,1,0:T(8,128)(2,1)} %spread.3), calls=%async_computation | async-start | bytes 2097152 | tf_op jit(solution)/shard_map/all_to_all | solution.py:133
  10.4 9.5 %collective-permute-start = (bf16[1,32,4096]{2,1,0:T(8,128)(2,1)S(1)}, bf16[1,32,4096]{2,1,0:T(8,128)(2,1)S(1)}, u32[]{:S(2)}, u32[]{:S(2)}) collective-permute-start(bf16[1,32,4096]{2,1,0:T(8,128)(2,1)S(1)} %constant_dynamic-slice_fusion.3), channel_id=1, source_target_pairs={{0,32},{16,112},{32,64},{48,16},{64,96},{80,48},{96,0},{112,80},{1... | collective-permute-start | bytes 786440 | tf_op jit(solution)/shard_map/ppermute | solution.py:139
  13.9 10.8 %collective-permute-start.1 = (bf16[1,32,4096]{2,1,0:T(8,128)(2,1)S(1)}, bf16[1,32,4096]{2,1,0:T(8,128)(2,1)S(1)}, u32[]{:S(2)}, u32[]{:S(2)}) collective-permute-start(bf16[1,32,4096]{2,1,0:T(8,128)(2,1)S(1)} %constant_dynamic-slice_fusion.3), channel_id=1, source_target_pairs={{0,96},{16,48},{32,0},{48,80},{64,32},{80,112},{96,64},{112,16},{1... | collective-permute-start | bytes 786440 | tf_op jit(solution)/shard_map/ppermute | solution.py:140
  19.9 9.6 %collective-permute-start.2 = (bf16[1,32,4096]{2,1,0:T(8,128)(2,1)S(1)}, bf16[1,32,4096]{2,1,0:T(8,128)(2,1)}, u32[]{:S(2)}, u32[]{:S(2)}) collective-permute-start(bf16[1,32,4096]{2,1,0:T(8,128)(2,1)S(1)} %collective-permute-done), channel_id=1, source_target_pairs={{0,32},{16,112},{32,64},{48,16},{64,96},{80,48},{96,0},{112,80},{1... | collective-permute-start | bytes 786440 | tf_op jit(solution)/shard_map/ppermute | solution.py:140
  36.2 17.7 %collective-permute-start.5 = (bf16[3,32,4096]{2,1,0:T(8,128)(2,1)}, bf16[3,32,4096]{2,1,0:T(8,128)(2,1)}, u32[]{:S(2)}, u32[]{:S(2)}) collective-permute-start(bf16[3,32,4096]{2,1,0:T(8,128)(2,1)} %pad_maximum_fusion.1), channel_id=1, source_target_pairs={{0,32},{16,112},{32,64},{48,16},{64,96},{80,48},{96,0},{112,80},{1... | collective-permute-start | bytes 2359304 | tf_op jit(solution)/shard_map/ppermute | solution.py:139
  39.6 41.0 %all-to-all-start.1 = ((bf16[4,48,4096]{2,1,0:T(8,128)(2,1)}), bf16[4,48,4096]{2,1,0:T(8,128)(2,1)S(1)}, u32[]{:S(2)}, u32[]{:S(2)}) async-start(bf16[4,48,4096]{2,1,0:T(8,128)(2,1)} %spread.2), calls=%async_computation.1 | async-start | bytes 3145728 | tf_op jit(solution)/shard_map/all_to_all | solution.py:144
  43.2 18.5 %collective-permute-start.7 = (bf16[3,32,4096]{2,1,0:T(8,128)(2,1)}, bf16[3,32,4096]{2,1,0:T(8,128)(2,1)}, u32[]{:S(2)}, u32[]{:S(2)}) collective-permute-start(bf16[3,32,4096]{2,1,0:T(8,128)(2,1)} %pad_maximum_fusion.1), channel_id=1, source_target_pairs={{0,96},{16,48},{32,0},{48,80},{64,32},{80,112},{96,64},{112,16},{1... | collective-permute-start | bytes 2359304 | tf_op jit(solution)/shard_map/ppermute | solution.py:140
  53.9 15.7 %collective-permute-start.9 = (bf16[3,32,4096]{2,1,0:T(8,128)(2,1)}, bf16[3,32,4096]{2,1,0:T(8,128)(2,1)}, u32[]{:S(2)}, u32[]{:S(2)}) collective-permute-start(bf16[3,32,4096]{2,1,0:T(8,128)(2,1)} %collective-permute-done.5.refs_4_), channel_id=1, source_target_pairs={{0,32},{16,112},{32,64},{48,16},{64,96},{80,48},{96,0},{112,80},{1... | collective-permute-start | bytes 2359304 | tf_op jit(solution)/shard_map/ppermute | solution.py:140
  57.3 14.4 %collective-permute-start.3 = (bf16[4,32,4096]{2,1,0:T(8,128)(2,1)S(1)}, bf16[4,32,4096]{2,1,0:T(8,128)(2,1)}, u32[]{:S(2)}, u32[]{:S(2)}) collective-permute-start(bf16[4,32,4096]{2,1,0:T(8,128)(2,1)S(1)} %all-to-all-done.refs_0_), channel_id=1, source_target_pairs={{0,16},{16,0},{1,17},{17,1},{2,18},{18,2},{3,19},{19,3},{4,20},{20... | collective-permute-start | bytes 3145736 | tf_op jit(solution)/shard_map/ppermute | solution.py:136
  59.3 12.5 %collective-permute-start.4 = (bf16[3,32,4096]{2,1,0:T(8,128)(2,1)S(1)}, bf16[3,32,4096]{2,1,0:T(8,128)(2,1)}, u32[]{:S(2)}, u32[]{:S(2)}) collective-permute-start(bf16[3,32,4096]{2,1,0:T(8,128)(2,1)S(1)} %pad_maximum_fusion.refs_1_), channel_id=1, source_target_pairs={{0,16},{16,0},{1,17},{17,1},{2,18},{18,2},{3,19},{19,3},{4,20},{20... | collective-permute-start | bytes 2359304 | tf_op jit(solution)/shard_map/ppermute | solution.py:136
  61.7 10.1 %collective-permute-start.8 = (bf16[3,32,4096]{2,1,0:T(8,128)(2,1)}, bf16[3,32,4096]{2,1,0:T(8,128)(2,1)}, u32[]{:S(2)}, u32[]{:S(2)}) collective-permute-start(bf16[3,32,4096]{2,1,0:T(8,128)(2,1)} %collective-permute-done.7.refs_6_), channel_id=1, source_target_pairs={{0,16},{16,0},{1,17},{17,1},{2,18},{18,2},{3,19},{19,3},{4,20},{20... | collective-permute-start | bytes 2359304 | tf_op jit(solution)/shard_map/ppermute | solution.py:136
  63.6 8.1 %collective-permute-start.6 = (bf16[3,32,4096]{2,1,0:T(8,128)(2,1)}, bf16[3,32,4096]{2,1,0:T(8,128)(2,1)}, u32[]{:S(2)}, u32[]{:S(2)}) collective-permute-start(bf16[3,32,4096]{2,1,0:T(8,128)(2,1)} %collective-permute-done.5.refs_4_), channel_id=1, source_target_pairs={{0,16},{16,0},{1,17},{17,1},{2,18},{18,2},{3,19},{19,3},{4,20},{20... | collective-permute-start | bytes 2359304 | tf_op jit(solution)/shard_map/ppermute | solution.py:136
  69.6 11.1 %collective-permute-start.10 = (bf16[3,32,4096]{2,1,0:T(8,128)(2,1)}, bf16[3,32,4096]{2,1,0:T(8,128)(2,1)}, u32[]{:S(2)}, u32[]{:S(2)}) collective-permute-start(bf16[3,32,4096]{2,1,0:T(8,128)(2,1)} %collective-permute-done.9.refs_8_), channel_id=1, source_target_pairs={{0,16},{16,0},{1,17},{17,1},{2,18},{18,2},{3,19},{19,3},{4,20},{20... | collective-permute-start | bytes 2359304 | tf_op jit(solution)/shard_map/ppermute | solution.py:136
  112.9 9.9 %collective-permute-start.11 = (f32[16,256]{1,0:T(8,128)S(1)}, f32[16,256]{1,0:T(8,128)S(1)}, u32[]{:S(2)}, u32[]{:S(2)}) collective-permute-start(f32[16,256]{1,0:T(8,128)S(1)} %reduce_sum.27), channel_id=1, source_target_pairs={{0,8},{8,0},{1,9},{9,1},{2,10},{10,2},{3,11},{11,3},{4,12},{12,4},... | collective-permute-start | bytes 49160 | tf_op jit(solution)/shard_map/ppermute | solution.py:157

commit v6 on v5

--- a/solution.py
+++ b/solution.py
@@ -50,7 +50,7 @@
     for i in range(2, m):
         held.append(late.at[pl.ds(starts[i] - starts[2], sizes[i])])
         copies.append(pltpu.make_async_copy(refs[i], held[i], sem.at[i - 2]))
-    for copy in copies[2:]:
+    for copy in copies[2:6]:
         copy.start()
     s = s_ref[...].reshape(192, DEPTH)
     ss = lax.dot_general(s, s, nt, preferred_element_type=F32)
@@ -95,6 +95,9 @@
         both = (both.reshape(2 * n, 8, 256) + spare[None]).reshape(n, 2, 8, 256)
         for j in range(n):
             out[pl.ds(place[a + j], 1), pl.ds(place[sum(sizes) + a + j], 2)] = both[j : j + 1]
+        if a == 0:
+            for copy in copies[6:]:
+                copy.start()
 
 
 def products(at, blocks, s):

time: 136 us -> 136 us (level)
  no operation moved by 1% of the time
where the time goes in v6:
time: 136 us; the launch traced here: 135 us
  starting transfers between devices  50.5 us (37%)
  blocking collectives  36 us (26%)
  waiting for transfers between devices  33.1 us (24%)
  Pallas kernels  10.4 us (8%)
  local copies, waits for them, and re-layouts  2.44 us (2%)
  other arithmetic  2.37 us (2%)
    all_to_all x1, blocking collectives, per_device(): parts = a2a(pieces.reshape(32, 16, 256), ('row', 'y'))  25.3 us
    all_to_all x1, blocking collectives, per_device(): full = a2a(jnp.broadcast_to(block[None], (8, 16, 96)), 'y')  10.7 us
    ppermute x5, starting transfers between devices, swap(): return lax.ppermute(block, 'core', SWAP)  10.6 us
    ppermute x2, waiting for transfers between devices, around(): first = lax.ppermute(own, ('x', 'core'), AHEAD)  9.45 us
    all_to_all x1, waiting for transfers between devices, per_device(): s = a2a(s, 'row')  8.86 us
    ppermute x2, waiting for transfers between devices, around(): lax.ppermute(first, ('x', 'core'), AHEAD)  8.46 us
    ppermute x1, starting transfers between devices, per_device(): total = total + lax.ppermute(total, 'zhi', SWAP)  8.23 us
    all_to_all x1, starting transfers between devices, per_device(): t = a2a(held, 'row')  7.39 us
  transfers between devices with their start and end apart: 14, of which 7 were waited for; matrix products, arithmetic and copies ran while one was open for 2% of the time, Pallas kernels for 1%

profile of v6, /device:TPU:8, one launch (start us, length us, event | category | flops | bytes accessed | tf_op | source)
XLA Modules:
  0.0 135.1 jit_solution(1331042360061516992)
XLA Ops:
  0.0 2.1 %spread.3 = bf16[4,32,4096]{2,1,0:T(8,128)(2,1)} custom-call(bf16[16,2,16384]{2,1,0:T(2,128)(2,1)} %states.3), custom_call_target="tpu_custom_call" | custom-call | tf_op jit(solution)/shard_map/spread/pallas_call | solution.py:33
  2.1 7.4 %all-to-all-start = ((bf16[4,32,4096]{2,1,0:T(8,128)(2,1)}), bf16[4,32,4096]{2,1,0:T(8,128)(2,1)S(1)}, u32[]{:S(2)}, u32[]{:S(2)}) async-start(bf16[4,32,4096]{2,1,0:T(8,128)(2,1)} %spread.3), calls=%async_computation | async-start | bytes 2097152 | tf_op jit(solution)/shard_map/all_to_all | solution.py:136
  10.4 3.4 %collective-permute-start = (bf16[1,32,4096]{2,1,0:T(8,128)(2,1)S(1)}, bf16[1,32,4096]{2,1,0:T(8,128)(2,1)S(1)}, u32[]{:S(2)}, u32[]{:S(2)}) collective-permute-start(bf16[1,32,4096]{2,1,0:T(8,128)(2,1)S(1)} %constant_dynamic-slice_fusion.3), channel_id=1, source_target_pairs={{0,32},{16,112},{32,64},{48,16},{64,96},{80,48},{96,0},{112,80},{1... | collective-permute-start | bytes 786440 | tf_op jit(solution)/shard_map/ppermute | solution.py:142
  13.9 3.7 %collective-permute-start.1 = (bf16[1,32,4096]{2,1,0:T(8,128)(2,1)S(1)}, bf16[1,32,4096]{2,1,0:T(8,128)(2,1)S(1)}, u32[]{:S(2)}, u32[]{:S(2)}) collective-permute-start(bf16[1,32,4096]{2,1,0:T(8,128)(2,1)S(1)} %constant_dynamic-slice_fusion.3), channel_id=1, source_target_pairs={{0,96},{16,48},{32,0},{48,80},{64,32},{80,112},{96,64},{112,16},{1... | collective-permute-start | bytes 786440 | tf_op jit(solution)/shard_map/ppermute | solution.py:143
  17.5 2.4 %collective-permute-done = bf16[1,32,4096]{2,1,0:T(8,128)(2,1)S(1)} collective-permute-done((bf16[1,32,4096]{2,1,0:T(8,128)(2,1)S(1)}, bf16[1,32,4096]{2,1,0:T(8,128)(2,1)S(1)}, u32[]{:S(2)}, u32[]{:S(2)}) %collective-permute-start) | collective-permute-done | bytes 262176 | tf_op jit(solution)/shard_map/ppermute | solution.py:142
  19.9 3.3 %collective-permute-start.2 = (bf16[1,32,4096]{2,1,0:T(8,128)(2,1)S(1)}, bf16[1,32,4096]{2,1,0:T(8,128)(2,1)}, u32[]{:S(2)}, u32[]{:S(2)}) collective-permute-start(bf16[1,32,4096]{2,1,0:T(8,128)(2,1)S(1)} %collective-permute-done), channel_id=1, source_target_pairs={{0,32},{16,112},{32,64},{48,16},{64,96},{80,48},{96,0},{112,80},{1... | collective-permute-start | bytes 786440 | tf_op jit(solution)/shard_map/ppermute | solution.py:143
  24.6 4.9 %collective-permute-done.2 = bf16[1,32,4096]{2,1,0:T(8,128)(2,1)} collective-permute-done((bf16[1,32,4096]{2,1,0:T(8,128)(2,1)S(1)}, bf16[1,32,4096]{2,1,0:T(8,128)(2,1)}, u32[]{:S(2)}, u32[]{:S(2)}) %collective-permute-start.2) | collective-permute-done | bytes 262176 | tf_op jit(solution)/shard_map/ppermute | solution.py:143
  30.6 4.6 %all-to-all-done.refs_0_ = bf16[4,32,4096]{2,1,0:T(8,128)(2,1)S(1)} async-done(((bf16[4,32,4096]{2,1,0:T(8,128)(2,1)}), bf16[4,32,4096]{2,1,0:T(8,128)(2,1)S(1)}, u32[]{:S(2)}, u32[]{:S(2)}) %all-to-all-start) | async-done | bytes 1048608 | tf_op jit(solution)/shard_map/all_to_all | solution.py:136
  36.2 3.4 %collective-permute-start.5 = (bf16[3,32,4096]{2,1,0:T(8,128)(2,1)}, bf16[3,32,4096]{2,1,0:T(8,128)(2,1)}, u32[]{:S(2)}, u32[]{:S(2)}) collective-permute-start(bf16[3,32,4096]{2,1,0:T(8,128)(2,1)} %pad_maximum_fusion.1), channel_id=1, source_target_pairs={{0,32},{16,112},{32,64},{48,16},{64,96},{80,48},{96,0},{112,80},{1... | collective-permute-start | bytes 2359304 | tf_op jit(solution)/shard_map/ppermute | solution.py:142
  39.6 3.6 %all-to-all-start.1 = ((bf16[4,48,4096]{2,1,0:T(8,128)(2,1)}), bf16[4,48,4096]{2,1,0:T(8,128)(2,1)S(1)}, u32[]{:S(2)}, u32[]{:S(2)}) async-start(bf16[4,48,4096]{2,1,0:T(8,128)(2,1)} %spread.2), calls=%async_computation.1 | async-start | bytes 3145728 | tf_op jit(solution)/shard_map/all_to_all | solution.py:147
  43.2 3.7 %collective-permute-start.7 = (bf16[3,32,4096]{2,1,0:T(8,128)(2,1)}, bf16[3,32,4096]{2,1,0:T(8,128)(2,1)}, u32[]{:S(2)}, u32[]{:S(2)}) collective-permute-start(bf16[3,32,4096]{2,1,0:T(8,128)(2,1)} %pad_maximum_fusion.1), channel_id=1, source_target_pairs={{0,96},{16,48},{32,0},{48,80},{64,32},{80,112},{96,64},{112,16},{1... | collective-permute-start | bytes 2359304 | tf_op jit(solution)/shard_map/ppermute | solution.py:143
  46.9 7.0 %collective-permute-done.5.refs_4_ = bf16[3,32,4096]{2,1,0:T(8,128)(2,1)} collective-permute-done((bf16[3,32,4096]{2,1,0:T(8,128)(2,1)}, bf16[3,32,4096]{2,1,0:T(8,128)(2,1)}, u32[]{:S(2)}, u32[]{:S(2)}) %collective-permute-start.5) | collective-permute-done | bytes 786464 | tf_op jit(solution)/shard_map/ppermute | solution.py:142
  53.9 3.4 %collective-permute-start.9 = (bf16[3,32,4096]{2,1,0:T(8,128)(2,1)}, bf16[3,32,4096]{2,1,0:T(8,128)(2,1)}, u32[]{:S(2)}, u32[]{:S(2)}) collective-permute-start(bf16[3,32,4096]{2,1,0:T(8,128)(2,1)} %collective-permute-done.5.refs_4_), channel_id=1, source_target_pairs={{0,32},{16,112},{32,64},{48,16},{64,96},{80,48},{96,0},{112,80},{1... | collective-permute-start | bytes 2359304 | tf_op jit(solution)/shard_map/ppermute | solution.py:143
  57.3 1.9 %collective-permute-start.3 = (bf16[4,32,4096]{2,1,0:T(8,128)(2,1)S(1)}, bf16[4,32,4096]{2,1,0:T(8,128)(2,1)}, u32[]{:S(2)}, u32[]{:S(2)}) collective-permute-start(bf16[4,32,4096]{2,1,0:T(8,128)(2,1)S(1)} %all-to-all-done.refs_0_), channel_id=1, source_target_pairs={{0,16},{16,0},{1,17},{17,1},{2,18},{18,2},{3,19},{19,3},{4,20},{20... | collective-permute-start | bytes 3145736 | tf_op jit(solution)/shard_map/ppermute | solution.py:139
  59.3 2.4 %collective-permute-start.4 = (bf16[3,32,4096]{2,1,0:T(8,128)(2,1)S(1)}, bf16[3,32,4096]{2,1,0:T(8,128)(2,1)}, u32[]{:S(2)}, u32[]{:S(2)}) collective-permute-start(bf16[3,32,4096]{2,1,0:T(8,128)(2,1)S(1)} %pad_maximum_fusion.refs_1_), channel_id=1, source_target_pairs={{0,16},{16,0},{1,17},{17,1},{2,18},{18,2},{3,19},{19,3},{4,20},{20... | collective-permute-start | bytes 2359304 | tf_op jit(solution)/shard_map/ppermute | solution.py:139
  61.7 1.9 %collective-permute-start.8 = (bf16[3,32,4096]{2,1,0:T(8,128)(2,1)}, bf16[3,32,4096]{2,1,0:T(8,128)(2,1)}, u32[]{:S(2)}, u32[]{:S(2)}) collective-permute-start(bf16[3,32,4096]{2,1,0:T(8,128)(2,1)} %collective-permute-done.7.refs_6_), channel_id=1, source_target_pairs={{0,16},{16,0},{1,17},{17,1},{2,18},{18,2},{3,19},{19,3},{4,20},{20... | collective-permute-start | bytes 2359304 | tf_op jit(solution)/shard_map/ppermute | solution.py:139
  63.6 2.4 %collective-permute-start.6 = (bf16[3,32,4096]{2,1,0:T(8,128)(2,1)}, bf16[3,32,4096]{2,1,0:T(8,128)(2,1)}, u32[]{:S(2)}, u32[]{:S(2)}) collective-permute-start(bf16[3,32,4096]{2,1,0:T(8,128)(2,1)} %collective-permute-done.5.refs_4_), channel_id=1, source_target_pairs={{0,16},{16,0},{1,17},{17,1},{2,18},{18,2},{3,19},{19,3},{4,20},{20... | collective-permute-start | bytes 2359304 | tf_op jit(solution)/shard_map/ppermute | solution.py:139
  66.0 3.5 %collective-permute-done.9.refs_8_ = bf16[3,32,4096]{2,1,0:T(8,128)(2,1)} collective-permute-done((bf16[3,32,4096]{2,1,0:T(8,128)(2,1)}, bf16[3,32,4096]{2,1,0:T(8,128)(2,1)}, u32[]{:S(2)}, u32[]{:S(2)}) %collective-permute-start.9) | collective-permute-done | bytes 786464 | tf_op jit(solution)/shard_map/ppermute | solution.py:143
  69.6 1.9 %collective-permute-start.10 = (bf16[3,32,4096]{2,1,0:T(8,128)(2,1)}, bf16[3,32,4096]{2,1,0:T(8,128)(2,1)}, u32[]{:S(2)}, u32[]{:S(2)}) collective-permute-start(bf16[3,32,4096]{2,1,0:T(8,128)(2,1)} %collective-permute-done.9.refs_8_), channel_id=1, source_target_pairs={{0,16},{16,0},{1,17},{17,1},{2,18},{18,2},{3,19},{19,3},{4,20},{20... | collective-permute-start | bytes 2359304 | tf_op jit(solution)/shard_map/ppermute | solution.py:139
  71.8 8.9 %all-to-all-done.1.refs_10_ = bf16[4,48,4096]{2,1,0:T(8,128)(2,1)S(1)} async-done(((bf16[4,48,4096]{2,1,0:T(8,128)(2,1)}), bf16[4,48,4096]{2,1,0:T(8,128)(2,1)S(1)}, u32[]{:S(2)}, u32[]{:S(2)}) %all-to-all-start.1) | async-done | bytes 1572896 | tf_op jit(solution)/shard_map/all_to_all | solution.py:147
  80.6 6.9 %products.1 = f32[4,16,8,256]{3,2,1,0:T(8,128)S(1)} custom-call(s32[64]{0:T(128)S(1)} %stack.38.place, bf16[4,32,4096]{2,1,0:T(8,128)(2,1)S(1)} %all-to-all-done.refs_0_, bf16[3,32,4096]{2,1,0:T(8,128)(2,1)S(1)} %pad_maximum_fusion.refs_1_, bf16[4,32,4096]{2,1,0:T(8,128)(2,1)} %collective-permute-done.3.refs_2_, ...), custom_call_target="tpu_custom_call" | custom-call | flops 1610612736 | bytes 8388608 | tf_op jit(solution)/shard_map/products/pallas_call | solution.py:107
  87.6 25.3 %all_to_all.20 = f32[32,16,256]{2,1,0:T(8,128)S(1)} all-to-all(f32[32,16,256]{2,1,0:T(8,128)S(1)} %bitcast.15), channel_id=1, replica_groups=mesh['row'=4,'x'=4,'core'=2,'zhi'=2,'y'=8] {'row','y'}, dimensions={0} | all-to-all | bytes 1048576 | tf_op jit(solution)/shard_map/all_to_all | solution.py:158
  112.9 8.2 %collective-permute-start.11 = (f32[16,256]{1,0:T(8,128)S(1)}, f32[16,256]{1,0:T(8,128)S(1)}, u32[]{:S(2)}, u32[]{:S(2)}) collective-permute-start(f32[16,256]{1,0:T(8,128)S(1)} %reduce_sum.27), channel_id=1, source_target_pairs={{0,8},{8,0},{1,9},{9,1},{2,10},{10,2},{3,11},{11,3},{4,12},{12,4},... | collective-permute-start | bytes 49160 | tf_op jit(solution)/shard_map/ppermute | solution.py:160
  123.8 10.7 %all_to_all.21 = f32[8,16,96]{2,1,0:T(8,128)S(1)} all-to-all(f32[8,16,96]{2,1,0:T(8,128)S(1)} %broadcast_in_dim.2), channel_id=1, replica_groups=mesh['row'=4,'x'=4,'core'=2,'zhi'=2,'y'=8] {'y'}, dimensions={0} | all-to-all | bytes 98304 | tf_op jit(solution)/shard_map/all_to_all | solution.py:166
  (29 shorter events, 7.9 us)
Async XLA Ops:
  2.1 21.2 %copy-start = (bf16[24,2,16384]{2,1,0:T(2,128)(2,1)S(1)}, bf16[24,2,16384]{2,1,0:T(2,128)(2,1)}, u32[]{:S(2)}) copy-start(bf16[24,2,16384]{2,1,0:T(2,128)(2,1)} %states.2) | copy-start | bytes 4718596
  2.1 33.1 %all-to-all-start = ((bf16[4,32,4096]{2,1,0:T(8,128)(2,1)}), bf16[4,32,4096]{2,1,0:T(8,128)(2,1)S(1)}, u32[]{:S(2)}, u32[]{:S(2)}) async-start(bf16[4,32,4096]{2,1,0:T(8,128)(2,1)} %spread.3), calls=%async_computation | async-start | bytes 2097152 | tf_op jit(solution)/shard_map/all_to_all | solution.py:136
  10.4 9.5 %collective-permute-start = (bf16[1,32,4096]{2,1,0:T(8,128)(2,1)S(1)}, bf16[1,32,4096]{2,1,0:T(8,128)(2,1)S(1)}, u32[]{:S(2)}, u32[]{:S(2)}) collective-permute-start(bf16[1,32,4096]{2,1,0:T(8,128)(2,1)S(1)} %constant_dynamic-slice_fusion.3), channel_id=1, source_target_pairs={{0,32},{16,112},{32,64},{48,16},{64,96},{80,48},{96,0},{112,80},{1... | collective-permute-start | bytes 786440 | tf_op jit(solution)/shard_map/ppermute | solution.py:142
  13.9 10.8 %collective-permute-start.1 = (bf16[1,32,4096]{2,1,0:T(8,128)(2,1)S(1)}, bf16[1,32,4096]{2,1,0:T(8,128)(2,1)S(1)}, u32[]{:S(2)}, u32[]{:S(2)}) collective-permute-start(bf16[1,32,4096]{2,1,0:T(8,128)(2,1)S(1)} %constant_dynamic-slice_fusion.3), channel_id=1, source_target_pairs={{0,96},{16,48},{32,0},{48,80},{64,32},{80,112},{96,64},{112,16},{1... | collective-permute-start | bytes 786440 | tf_op jit(solution)/shard_map/ppermute | solution.py:143
  19.9 9.6 %collective-permute-start.2 = (bf16[1,32,4096]{2,1,0:T(8,128)(2,1)S(1)}, bf16[1,32,4096]{2,1,0:T(8,128)(2,1)}, u32[]{:S(2)}, u32[]{:S(2)}) collective-permute-start(bf16[1,32,4096]{2,1,0:T(8,128)(2,1)S(1)} %collective-permute-done), channel_id=1, source_target_pairs={{0,32},{16,112},{32,64},{48,16},{64,96},{80,48},{96,0},{112,80},{1... | collective-permute-start | bytes 786440 | tf_op jit(solution)/shard_map/ppermute | solution.py:143
  36.2 17.7 %collective-permute-start.5 = (bf16[3,32,4096]{2,1,0:T(8,128)(2,1)}, bf16[3,32,4096]{2,1,0:T(8,128)(2,1)}, u32[]{:S(2)}, u32[]{:S(2)}) collective-permute-start(bf16[3,32,4096]{2,1,0:T(8,128)(2,1)} %pad_maximum_fusion.1), channel_id=1, source_target_pairs={{0,32},{16,112},{32,64},{48,16},{64,96},{80,48},{96,0},{112,80},{1... | collective-permute-start | bytes 2359304 | tf_op jit(solution)/shard_map/ppermute | solution.py:142
  39.6 41.0 %all-to-all-start.1 = ((bf16[4,48,4096]{2,1,0:T(8,128)(2,1)}), bf16[4,48,4096]{2,1,0:T(8,128)(2,1)S(1)}, u32[]{:S(2)}, u32[]{:S(2)}) async-start(bf16[4,48,4096]{2,1,0:T(8,128)(2,1)} %spread.2), calls=%async_computation.1 | async-start | bytes 3145728 | tf_op jit(solution)/shard_map/all_to_all | solution.py:147
  43.2 18.5 %collective-permute-start.7 = (bf16[3,32,4096]{2,1,0:T(8,128)(2,1)}, bf16[3,32,4096]{2,1,0:T(8,128)(2,1)}, u32[]{:S(2)}, u32[]{:S(2)}) collective-permute-start(bf16[3,32,4096]{2,1,0:T(8,128)(2,1)} %pad_maximum_fusion.1), channel_id=1, source_target_pairs={{0,96},{16,48},{32,0},{48,80},{64,32},{80,112},{96,64},{112,16},{1... | collective-permute-start | bytes 2359304 | tf_op jit(solution)/shard_map/ppermute | solution.py:143
  53.9 15.7 %collective-permute-start.9 = (bf16[3,32,4096]{2,1,0:T(8,128)(2,1)}, bf16[3,32,4096]{2,1,0:T(8,128)(2,1)}, u32[]{:S(2)}, u32[]{:S(2)}) collective-permute-start(bf16[3,32,4096]{2,1,0:T(8,128)(2,1)} %collective-permute-done.5.refs_4_), channel_id=1, source_target_pairs={{0,32},{16,112},{32,64},{48,16},{64,96},{80,48},{96,0},{112,80},{1... | collective-permute-start | bytes 2359304 | tf_op jit(solution)/shard_map/ppermute | solution.py:143
  57.3 14.4 %collective-permute-start.3 = (bf16[4,32,4096]{2,1,0:T(8,128)(2,1)S(1)}, bf16[4,32,4096]{2,1,0:T(8,128)(2,1)}, u32[]{:S(2)}, u32[]{:S(2)}) collective-permute-start(bf16[4,32,4096]{2,1,0:T(8,128)(2,1)S(1)} %all-to-all-done.refs_0_), channel_id=1, source_target_pairs={{0,16},{16,0},{1,17},{17,1},{2,18},{18,2},{3,19},{19,3},{4,20},{20... | collective-permute-start | bytes 3145736 | tf_op jit(solution)/shard_map/ppermute | solution.py:139
  59.3 12.5 %collective-permute-start.4 = (bf16[3,32,4096]{2,1,0:T(8,128)(2,1)S(1)}, bf16[3,32,4096]{2,1,0:T(8,128)(2,1)}, u32[]{:S(2)}, u32[]{:S(2)}) collective-permute-start(bf16[3,32,4096]{2,1,0:T(8,128)(2,1)S(1)} %pad_maximum_fusion.refs_1_), channel_id=1, source_target_pairs={{0,16},{16,0},{1,17},{17,1},{2,18},{18,2},{3,19},{19,3},{4,20},{20... | collective-permute-start | bytes 2359304 | tf_op jit(solution)/shard_map/ppermute | solution.py:139
  61.7 10.1 %collective-permute-start.8 = (bf16[3,32,4096]{2,1,0:T(8,128)(2,1)}, bf16[3,32,4096]{2,1,0:T(8,128)(2,1)}, u32[]{:S(2)}, u32[]{:S(2)}) collective-permute-start(bf16[3,32,4096]{2,1,0:T(8,128)(2,1)} %collective-permute-done.7.refs_6_), channel_id=1, source_target_pairs={{0,16},{16,0},{1,17},{17,1},{2,18},{18,2},{3,19},{19,3},{4,20},{20... | collective-permute-start | bytes 2359304 | tf_op jit(solution)/shard_map/ppermute | solution.py:139
  63.6 8.1 %collective-permute-start.6 = (bf16[3,32,4096]{2,1,0:T(8,128)(2,1)}, bf16[3,32,4096]{2,1,0:T(8,128)(2,1)}, u32[]{:S(2)}, u32[]{:S(2)}) collective-permute-start(bf16[3,32,4096]{2,1,0:T(8,128)(2,1)} %collective-permute-done.5.refs_4_), channel_id=1, source_target_pairs={{0,16},{16,0},{1,17},{17,1},{2,18},{18,2},{3,19},{19,3},{4,20},{20... | collective-permute-start | bytes 2359304 | tf_op jit(solution)/shard_map/ppermute | solution.py:139
  69.6 11.1 %collective-permute-start.10 = (bf16[3,32,4096]{2,1,0:T(8,128)(2,1)}, bf16[3,32,4096]{2,1,0:T(8,128)(2,1)}, u32[]{:S(2)}, u32[]{:S(2)}) collective-permute-start(bf16[3,32,4096]{2,1,0:T(8,128)(2,1)} %collective-permute-done.9.refs_8_), channel_id=1, source_target_pairs={{0,16},{16,0},{1,17},{17,1},{2,18},{18,2},{3,19},{19,3},{4,20},{20... | collective-permute-start | bytes 2359304 | tf_op jit(solution)/shard_map/ppermute | solution.py:139
  112.9 9.9 %collective-permute-start.11 = (f32[16,256]{1,0:T(8,128)S(1)}, f32[16,256]{1,0:T(8,128)S(1)}, u32[]{:S(2)}, u32[]{:S(2)}) collective-permute-start(f32[16,256]{1,0:T(8,128)S(1)} %reduce_sum.27), channel_id=1, source_target_pairs={{0,8},{8,0},{1,9},{9,1},{2,10},{10,2},{3,11},{11,3},{4,12},{12,4},... | collective-permute-start | bytes 49160 | tf_op jit(solution)/shard_map/ppermute | solution.py:160
